TPU v7x, 512 devices: a whole 4x8x8 slice. The times are simulated.
512 devices in a mesh: section: 16 (over x, y_hi, core), expert: 32 (over z, y_lo).
Axes of the slice: x: 4, y: 8 (y_hi: 2, y_lo: 4; y = y_hi * 4 + y_lo), z: 8, core: 2. Of those that a mesh axis runs over, the one named last changes fastest.
Arguments:
- hidden_fwd: bfloat16 [16, 2048, 1024], P('section', 'expert'), may hold values from -6 to 6
- hidden_bwd: bfloat16 [16, 2048, 1024], P('section', 'expert'), may hold values from -6 to 6
- mid_bwd: bfloat16 [16, 2048, 1024], P('section', 'expert'), may hold values from -6 to 6
- grads_in: bfloat16 [16, 2048, 1024], P('section', 'expert'), may hold values from -6 to 6
- memory_saved: bfloat16 [2048, 1024], P('expert'), may hold values from -6 to 6
- lengths: int32 [4, 64], P(None, 'expert'), may hold values from 1 to 32
- routes_fwd: int32 [16, 2048, 2], P('section', 'expert'), may hold values from 0 to 3, all different within a row; in each aligned block of 64 rows (0 to 63, 64 to 127, ..., all dimensions but the last counted through in order) at most 36 rows name the same one
- routes_bwd: int32 [16, 2048, 2], P('section', 'expert'), may hold values from 0 to 3, all different within a row; in each aligned block of 64 rows (0 to 63, 64 to 127, ..., all dimensions but the last counted through in order) at most 36 rows name the same one
- probs_fwd: float32 [16, 2048, 2], P('section', 'expert'), may hold values from 0.1 to 0.9
- probs_bwd: float32 [16, 2048, 2], P('section', 'expert'), may hold values from 0.1 to 0.9
- norm_gains: float32 [16, 2, 1024], P('section'), may hold values from 0.5 to 1.5
- w_in: bfloat16 [16, 1024, 16384], P('section', None, 'expert'), may hold values from -0.1875 to 0.1875
- w_out: bfloat16 [16, 16384, 1024], P('section', 'expert'), may hold values from -0.09375 to 0.09375
- w_query: bfloat16 [16, 1024, 512], P('section', 'expert'), may hold values from -0.1875 to 0.1875
- w_keyval: bfloat16 [16, 1024, 1024], P('section', 'expert'), may hold values from -0.1875 to 0.1875
- w_output: bfloat16 [16, 512, 1024], P('section', 'expert'), may hold values from -0.25 to 0.25
Outputs:
- passed_rows: bfloat16 [16, 2048, 1024], P('section', 'expert')
- passed_grads: bfloat16 [16, 2048, 1024], P('section', 'expert')
- memory_grad: bfloat16 [2048, 1024], P('expert')
Inputs may be any that keep to these rules, and one draw needn't show every extreme that they name: `routes_fwd`: in the 64 rows of one section and one device no expert is named by more than 36 rows; a row's two experts differ. `routes_bwd`: in the 64 rows of one section and one device no expert is named by more than 36 rows; a row's two experts differ.
All inputs are finite; a program needn't handle non-finite values.
Results may differ from a plain program's by a relative error of at most 0.024.
Values may be sent and summed in bfloat16 or wider, within the bound.
A program may use at most 64 MiB of HBM per device.

v0:
```python
import jax
import jax.numpy as jnp
from jax import lax
from jax.sharding import PartitionSpec as P

HEAD_DIM = 64
EXPERTS = 4
SEQ = 32
CAP = 36


EPS = 1e-05
ROOT_HALF = 0.7071067811865476
INV_ROOT_TWO_PI = 0.3989422804014327


def spread_2(value, axis, root):
    mine = lax.axis_index(axis) == root
    return lax.psum(jnp.where(mine, value, jnp.zeros_like(value)), axis)


def passed_along(block, axis, distance):
    devices = range(lax.axis_size(axis))
    route = [((i - distance) % len(devices), i) for i in devices]
    return lax.ppermute(block, axis, route)


def layer_norm(row_block, gain_row):
    values = row_block.astype(jnp.float32)
    center = values - jnp.mean(values, axis=-1, keepdims=True)
    spread = jnp.mean(center * center, axis=-1, keepdims=True)
    return center * lax.rsqrt(spread + EPS) * gain_row


def gelu_value(inputs):
    return 0.5 * inputs * (1.0 + lax.erf(inputs * ROOT_HALF))


def gelu_slope(inputs):
    return (
        0.5 * (1.0 + lax.erf(inputs * ROOT_HALF))
        + inputs * jnp.exp(-0.5 * inputs * inputs) * INV_ROOT_TWO_PI
    )


def row_lengths(sent_lens, row_count):
    sentence = jnp.arange(row_count) // SEQ
    sent_match = sentence[:, None] == jnp.arange(sent_lens.shape[0])[None, :]
    return jnp.sum(jnp.where(sent_match, sent_lens[None, :], 0), axis=1)


def cross_attend(middle, memory, src_len, gain_row, query_w, keyval_w, output_w):
    row_count = middle.shape[0]
    inner_width = query_w.shape[1]
    head_count = inner_width // HEAD_DIM
    normed = layer_norm(middle, gain_row).astype(jnp.bfloat16)
    query_rows = jnp.dot(normed, query_w, preferred_element_type=jnp.float32).astype(jnp.bfloat16)
    keyval = jnp.dot(memory, keyval_w, preferred_element_type=jnp.float32).astype(jnp.bfloat16)
    q_heads = query_rows.reshape(row_count, head_count, HEAD_DIM).astype(jnp.float32)
    k_heads = keyval[:, :inner_width].reshape(row_count, head_count, HEAD_DIM).astype(jnp.float32)
    v_heads = keyval[:, inner_width:].reshape(row_count, head_count, HEAD_DIM).astype(jnp.float32)
    scores = jnp.einsum("qhd,khd->hqk", q_heads, k_heads) * HEAD_DIM ** (-0.5)
    row_index = jnp.arange(row_count)
    sentence = row_index // SEQ
    key_len = row_lengths(src_len, row_count)
    allowed = (sentence[:, None] == sentence[None, :]) & (
        (row_index % SEQ)[None, :] < key_len[None, :]
    )
    raised = jnp.where(allowed[None], jnp.exp(scores), 0.0)
    weights = (raised / jnp.sum(raised, axis=-1, keepdims=True)).astype(jnp.bfloat16)
    mixed_heads = jnp.einsum("hqk,khd->qhd", weights.astype(jnp.float32), v_heads).astype(
        jnp.bfloat16
    )
    projected = jnp.dot(
        mixed_heads.reshape(row_count, inner_width), output_w, preferred_element_type=jnp.float32
    )
    return (middle.astype(jnp.float32) + projected).astype(jnp.bfloat16)


def slot_tables(routes, live):
    flat_routes = routes.reshape(-1)
    valid_rows = jnp.repeat(live, 2)
    onehot = ((flat_routes[:, None] == jnp.arange(EXPERTS)[None, :]) & valid_rows[:, None]).astype(
        jnp.int32
    )
    before = jnp.cumsum(onehot, axis=0) - onehot
    slot_index = jnp.sum(before * onehot, axis=1)
    slot_place = jnp.where(valid_rows, flat_routes * CAP + slot_index, -1)
    slot_table = slot_place[None, :] == jnp.arange(EXPERTS * CAP)[:, None]
    by_token = jnp.any(slot_table.reshape(EXPERTS * CAP, -1, 2), axis=2)
    return (slot_table, by_token)


def pack_rows(slot_table, row_block, slice_count):
    packed = jnp.dot(
        slot_table.astype(jnp.bfloat16), row_block, preferred_element_type=jnp.float32
    ).astype(jnp.bfloat16)
    packed = packed.reshape(EXPERTS, CAP, row_block.shape[1])
    return jnp.repeat(packed, slice_count, axis=0)


def gather_slots(returned, slot_weights, slice_count):
    model_width = returned.shape[2]
    summed = jnp.sum(
        returned.reshape(EXPERTS, slice_count, CAP, model_width), axis=1, dtype=jnp.float32
    )
    summed = summed.reshape(EXPERTS * CAP, model_width)
    return lax.dot_general(
        slot_weights,
        summed,
        (((0,), (0,)), ((), ())),
        precision=lax.Precision.HIGHEST,
        preferred_element_type=jnp.float32,
    )


def on_device(
    hidden_fwd,
    hidden_bwd,
    mid_bwd,
    grads_in,
    memory_saved,
    lengths,
    routes_fwd,
    routes_bwd,
    probs_fwd,
    probs_bwd,
    norm_gains,
    w_in,
    w_out,
    w_query,
    w_keyval,
    w_output,
):
    section_count = lax.axis_size("section")
    member_count = lax.axis_size("expert")
    slice_count = member_count // EXPERTS
    first_decoder = max(1, 3 * section_count // 16)
    is_decoder = lax.axis_index("section") >= first_decoder
    row_count = hidden_fwd.shape[1]
    model_width = hidden_fwd.shape[2]
    gain_moe = norm_gains[0, 0]
    gain_att = norm_gains[0, 1]
    up_slice = w_in[0]
    down_slice = w_out[0]
    query_full, keyval_full, output_full = (
        lax.all_gather(w_query, "expert", axis=1, tiled=True),
        lax.all_gather(w_keyval, "expert", axis=1, tiled=True),
        lax.all_gather(w_output, "expert", axis=1, tiled=True),
    )
    query_w = query_full[0]
    keyval_w = keyval_full[0]
    output_w = output_full[0]
    position = jnp.arange(row_count) % SEQ
    lens_fwd = jnp.where(is_decoder, lengths[1], lengths[0])
    lens_bwd = jnp.where(is_decoder, lengths[3], lengths[2])
    live_fwd = position < row_lengths(lens_fwd, row_count)
    live_bwd = position < row_lengths(lens_bwd, row_count)
    hidden_a = hidden_fwd[0]
    hidden_b = hidden_bwd[0]
    normed_a = layer_norm(hidden_a, gain_moe).astype(jnp.bfloat16)
    normed_b = layer_norm(hidden_b, gain_moe).astype(jnp.bfloat16)
    table_a, token_a = slot_tables(routes_fwd[0], live_fwd)
    table_b, token_b = slot_tables(routes_bwd[0], live_bwd)
    send_a = pack_rows(token_a, normed_a, slice_count)
    cotangent = grads_in[0]

    def attend_saved(mid_rows, mem_rows):
        return cross_attend(mid_rows, mem_rows, lengths[2], gain_att, query_w, keyval_w, output_w)

    _, attend_grad = jax.vjp(attend_saved, mid_bwd[0], memory_saved)
    grad_mid, grad_memory = attend_grad(cotangent)
    upstream = jnp.where(is_decoder, grad_mid, cotangent)
    memory_term = jnp.where(is_decoder, grad_memory.astype(jnp.float32), 0.0)
    sent_rows = (
        (probs_bwd[0][:, :, None] * upstream.astype(jnp.float32)[:, None, :])
        .reshape(2 * row_count, model_width)
        .astype(jnp.bfloat16)
    )
    send_x = pack_rows(token_b, normed_b, slice_count)
    send_d = pack_rows(table_b, sent_rows, slice_count)
    received = lax.all_to_all(send_a, "expert", split_axis=0, concat_axis=0, tiled=True)
    flat_rows = received.reshape(-1, model_width)
    units = gelu_value(jnp.dot(flat_rows, up_slice, preferred_element_type=jnp.float32)).astype(
        jnp.bfloat16
    )
    back_a = lax.all_to_all(
        jnp.dot(units, down_slice, preferred_element_type=jnp.float32)
        .astype(jnp.bfloat16)
        .reshape(received.shape),
        "expert",
        split_axis=0,
        concat_axis=0,
        tiled=True,
    )
    received = (
        lax.all_to_all(send_x, "expert", split_axis=0, concat_axis=0, tiled=True),
        lax.all_to_all(send_d, "expert", split_axis=0, concat_axis=0, tiled=True),
    )
    received_x = received[0]
    flat_x = received_x.reshape(-1, model_width)
    flat_d = received[1].reshape(-1, model_width)
    pre_act = jnp.dot(flat_x, up_slice, preferred_element_type=jnp.float32)
    through = lax.dot_general(
        flat_d, down_slice, (((1,), (1,)), ((), ())), preferred_element_type=jnp.float32
    )
    unit_grad = (through * gelu_slope(pre_act)).astype(jnp.bfloat16)
    dpart = lax.dot_general(
        unit_grad, up_slice, (((1,), (1,)), ((), ())), preferred_element_type=jnp.float32
    )
    back_b = lax.all_to_all(
        dpart.astype(jnp.bfloat16).reshape(received_x.shape),
        "expert",
        split_axis=0,
        concat_axis=0,
        tiled=True,
    )
    weight_a = jnp.sum(
        jnp.where(table_a.reshape(EXPERTS * CAP, row_count, 2), probs_fwd[0][None], 0.0), axis=2
    )
    mixed_a = gather_slots(back_a, weight_a, slice_count)
    middle_a = (hidden_a.astype(jnp.float32) + mixed_a).astype(jnp.bfloat16)
    memory = spread_2(middle_a, "section", first_decoder - 1)
    attended = cross_attend(middle_a, memory, lengths[0], gain_att, query_w, keyval_w, output_w)
    out_a = jnp.where(is_decoder, attended, middle_a)
    passed_rows = passed_along(out_a, "section", 1)
    grad_units = gather_slots(back_b, token_b.astype(jnp.float32), slice_count)

    def norm_only(inputs):
        return layer_norm(inputs, gain_moe)

    _, norm_grad = jax.vjp(norm_only, hidden_b.astype(jnp.float32))
    grad_hidden = (upstream.astype(jnp.float32) + norm_grad(grad_units)[0]).astype(jnp.bfloat16)
    passed_grads = passed_along(grad_hidden, "section", -1)
    memory_grad = lax.psum(memory_term.astype(jnp.bfloat16), "section")
    return (passed_rows[None], passed_grads[None], memory_grad)


def solution(mesh):
    return jax.shard_map(
        on_device,
        mesh=mesh,
        in_specs=(
            P("section", "expert", None),
            P("section", "expert", None),
            P("section", "expert", None),
            P("section", "expert", None),
            P("expert", None),
            P(None, "expert"),
            P("section", "expert", None),
            P("section", "expert", None),
            P("section", "expert", None),
            P("section", "expert", None),
            P("section", None, None),
            P("section", None, "expert"),
            P("section", "expert", None),
            P("section", "expert", None),
            P("section", "expert", None),
            P("section", "expert", None),
        ),
        out_specs=(P("section", "expert", None), P("section", "expert", None), P("expert", None)),
        check_vma=False,
    )
```

profile of v0, /device:TPU:55, one launch (start us, length us, event | category | flops | bytes accessed | tf_op | source)
XLA Modules:
  0.0 892.0 jit_solution(6547830053529157497)
XLA Ops:
  17.8 12.6 %all-to-all-start = ((bf16[32,36,1024]{2,1,0:T(8,128)(2,1)}), bf16[32,36,1024]{2,1,0:T(8,128)(2,1)}, u32[]{:S(2)}, u32[]{:S(2)}) async-start(bf16[32,36,1024]{2,1,0:T(8,128)(2,1)} %bitcast.176), calls=%async_computation | async-start | bytes 5242880 | tf_op jit(solution)/shard_map/all_to_all | solution.py:182
  34.0 68.3 %all-to-all-done = bf16[32,36,1024]{2,1,0:T(8,128)(2,1)} async-done(((bf16[32,36,1024]{2,1,0:T(8,128)(2,1)}), bf16[32,36,1024]{2,1,0:T(8,128)(2,1)}, u32[]{:S(2)}, u32[]{:S(2)}) %all-to-all-start) | async-done | bytes 2359328 | tf_op jit(solution)/shard_map/all_to_all | solution.py:182
  104.1 18.2 %all-to-all-start.3 = ((bf16[32,36,1024]{2,1,0:T(8,128)(2,1)}), bf16[32,36,1024]{2,1,0:T(8,128)(2,1)}, u32[]{:S(2)}, u32[]{:S(2)}) async-start(bf16[32,36,1024]{2,1,0:T(8,128)(2,1)} %bitcast.175), calls=%async_computation.3 | async-start | bytes 5242880 | tf_op jit(solution)/shard_map/all_to_all | solution.py:197
  124.8 58.2 %all-gather.6.cloned.1.call-done = bf16[1,1024,512]{2,1,0:T(8,128)(2,1)} async-done(((bf16[1,32,512]{2,1,0:T(8,128)(2,1)}), bf16[1,1024,512]{2,1,0:T(8,128)(2,1)}) %all-gather.6.cloned.1.call-update) | async-done | bytes 1048592 | tf_op jit(solution)/shard_map/all_gather | solution.py:147
  184.7 143.2 %all-gather.8.cloned.1.call-done = bf16[1,512,1024]{2,1,0:T(8,128)(2,1)} async-done(((bf16[1,16,1024]{2,1,0:T(8,128)(2,1)}), bf16[1,512,1024]{2,1,0:T(8,128)(2,1)}) %all-gather.8.cloned.1.call-update) | async-done | bytes 1048592 | tf_op jit(solution)/shard_map/all_gather | solution.py:149
  329.7 160.5 %all-gather.4.cloned.1.call-done = bf16[1,1024,1024]{2,1,0:T(8,128)(2,1)} async-done(((bf16[1,32,1024]{2,1,0:T(8,128)(2,1)}), bf16[1,1024,1024]{2,1,0:T(8,128)(2,1)}) %all-gather.4.cloned.1.call-update) | async-done | bytes 2097168 | tf_op jit(solution)/shard_map/all_gather | solution.py:148
  498.9 11.1 %all-to-all-start.2 = ((bf16[32,36,1024]{2,1,0:T(8,128)(2,1)}), bf16[32,36,1024]{2,1,0:T(8,128)(2,1)}, u32[]{:S(2)}, u32[]{:S(2)}) async-start(bf16[32,36,1024]{2,1,0:T(8,128)(2,1)} %bitcast.177), calls=%async_computation.2 | async-start | bytes 5242880 | tf_op jit(solution)/shard_map/all_to_all | solution.py:198
  510.0 4.2 reshape.387
  514.2 5.9 convolution_convert_fusion.1
  520.1 4.1 reshape.388
  524.2 44.2 %all-to-all-done.2 = bf16[32,36,1024]{2,1,0:T(8,128)(2,1)} async-done(((bf16[32,36,1024]{2,1,0:T(8,128)(2,1)}), bf16[32,36,1024]{2,1,0:T(8,128)(2,1)}, u32[]{:S(2)}, u32[]{:S(2)}) %all-to-all-start.2) | async-done | bytes 2359328 | tf_op jit(solution)/shard_map/all_to_all | solution.py:198
  568.5 14.6 %all-to-all-start.1 = ((bf16[32,36,1024]{2,1,0:T(8,128)(2,1)}), bf16[32,36,1024]{2,1,0:T(8,128)(2,1)}, u32[]{:S(2)}, u32[]{:S(2)}) async-start(bf16[32,36,1024]{2,1,0:T(8,128)(2,1)} %reshape.388), calls=%async_computation.1 | async-start | bytes 5242880 | tf_op jit(solution)/shard_map/all_to_all | solution.py:187
  583.0 4.1 reshape.404
  587.2 4.5 fusion.51
  591.6 4.1 reshape.401
  595.7 7.0 convolution_convert_fusion
  602.8 4.1 reshape.405
  606.8 39.3 %all-to-all-done.1 = bf16[32,36,1024]{2,1,0:T(8,128)(2,1)} async-done(((bf16[32,36,1024]{2,1,0:T(8,128)(2,1)}), bf16[32,36,1024]{2,1,0:T(8,128)(2,1)}, u32[]{:S(2)}, u32[]{:S(2)}) %all-to-all-start.1) | async-done | bytes 2359328 | tf_op jit(solution)/shard_map/all_to_all | solution.py:187
  646.2 9.3 %all-to-all-start.4 = ((bf16[32,36,1024]{2,1,0:T(8,128)(2,1)}), bf16[32,36,1024]{2,1,0:T(8,128)(2,1)}, u32[]{:S(2)}, u32[]{:S(2)}) async-start(bf16[32,36,1024]{2,1,0:T(8,128)(2,1)} %reshape.405), calls=%async_computation.4 | async-start | bytes 5242880 | tf_op jit(solution)/shard_map/all_to_all | solution.py:211
  662.7 3.2 convert_reduce_fusion.1
  672.9 186.8 %all-reduce.5.cloned.1.call-done = (bf16[64,1024]{1,0:T(8,128)(2,1)}, bf16[64,1024]{1,0:T(8,128)(2,1)}) async-done(((bf16[64,1024]{1,0:T(8,128)(2,1)}, bf16[64,1024]{1,0:T(8,128)(2,1)}), (bf16[64,1024]{1,0:T(8,128)(2,1)}, bf16[64,1024]{1,0:T(8,128)(2,1)})) %all-reduce.5.cloned.1.call-update) | async-done | bytes 262160 | tf_op jit(solution)/shard_map/psum | solution.py:19
  862.9 3.6 collective-permute-start
  866.5 2.3 convert_reduce_fusion
  871.7 11.8 %collective-permute-done.1 = bf16[64,1024]{1,0:T(8,128)(2,1)S(1)} collective-permute-done((bf16[64,1024]{1,0:T(8,128)(2,1)S(1)}, bf16[64,1024]{1,0:T(8,128)(2,1)S(1)}, u32[]{:S(2)}, u32[]{:S(2)}) %collective-permute-start.1) | collective-permute-done | bytes 131104 | tf_op jit(solution)/shard_map/ppermute | solution.py:25
  (202 shorter events, 52.2 us)
Async XLA Ops:
  7.2 507.1 %copy-start = (bf16[1,1024,512]{2,1,0:T(8,128)(2,1)S(1)}, bf16[1,1024,512]{2,1,0:T(8,128)(2,1)}, u32[]{:S(2)}) copy-start(bf16[1,1024,512]{2,1,0:T(8,128)(2,1)} %param.27) | copy-start | bytes 3145732
  7.2 175.8 %all-gather.6.cloned.1.call-start = ((), (), s32[]{:S(2)}) async-start(), calls=%async_computation.6 | async-start | bytes 1081344 | tf_op jit(solution)/shard_map/all_gather | solution.py:147
  14.7 168.3 %copy-start.19 = (f32[1,1,1024]{2,1,0:T(1,128)}, f32[1,1,1024]{2,1,0:T(1,128)S(1)}, u32[]{:S(2)}) copy-start(f32[1,1,1024]{2,1,0:T(1,128)S(1)} %get-tuple-element.17) | copy-start | bytes 12292
  17.8 84.4 %all-to-all-start = ((bf16[32,36,1024]{2,1,0:T(8,128)(2,1)}), bf16[32,36,1024]{2,1,0:T(8,128)(2,1)}, u32[]{:S(2)}, u32[]{:S(2)}) async-start(bf16[32,36,1024]{2,1,0:T(8,128)(2,1)} %bitcast.176), calls=%async_computation | async-start | bytes 5242880 | tf_op jit(solution)/shard_map/all_to_all | solution.py:182
  30.4 297.5 %all-gather.8.cloned.1.call-start = ((), (), s32[]{:S(2)}) async-start(), calls=%async_computation.7 | async-start | bytes 1081344 | tf_op jit(solution)/shard_map/all_gather | solution.py:149
  31.2 459.0 %all-gather.4.cloned.1.call-start = ((), (), s32[]{:S(2)}) async-start(), calls=%async_computation.5 | async-start | bytes 2162688 | tf_op jit(solution)/shard_map/all_gather | solution.py:148
  33.3 70.7 %copy-start.24 = (f32[64]{0:T(128)}, f32[64]{0:T(128)S(1)}, u32[]{:S(2)}) copy-start(f32[64]{0:T(128)S(1)} %broadcast_multiply_fusion) | copy-start | bytes 772
  33.5 70.5 %copy-start.37 = (f32[64]{0:T(128)}, f32[64]{0:T(128)S(1)}, u32[]{:S(2)}) copy-start(f32[64]{0:T(128)S(1)} %fusion.77) | copy-start | bytes 772
  33.6 70.5 %copy-start.27 = (f32[64]{0:T(128)}, f32[64]{0:T(128)S(1)}, u32[]{:S(2)}) copy-start(f32[64]{0:T(128)S(1)} %fusion.139) | copy-start | bytes 772
  104.1 223.8 %copy-start.9 = (bf16[1,64,1024]{2,1,0:T(8,128)(2,1)S(1)}, bf16[1,64,1024]{2,1,0:T(8,128)(2,1)}, u32[]{:S(2)}) copy-start(bf16[1,64,1024]{2,1,0:T(8,128)(2,1)} %param.19) | copy-start | bytes 393220
  104.1 393.0 %all-to-all-start.3 = ((bf16[32,36,1024]{2,1,0:T(8,128)(2,1)}), bf16[32,36,1024]{2,1,0:T(8,128)(2,1)}, u32[]{:S(2)}, u32[]{:S(2)}) async-start(bf16[32,36,1024]{2,1,0:T(8,128)(2,1)} %bitcast.175), calls=%async_computation.3 | async-start | bytes 5242880 | tf_op jit(solution)/shard_map/all_to_all | solution.py:197
  122.4 367.8 %copy-start.12 = (bf16[64,1024]{1,0:T(8,128)(2,1)S(1)}, bf16[64,1024]{1,0:T(8,128)(2,1)}, u32[]{:S(2)}) copy-start(bf16[64,1024]{1,0:T(8,128)(2,1)} %param.20) | copy-start | bytes 393220
  123.3 204.6 %copy-start.22 = (f32[64]{0:T(128)}, f32[64]{0:T(128)S(1)}, u32[]{:S(2)}) copy-start(f32[64]{0:T(128)S(1)} %broadcast_multiply_fusion.1) | copy-start | bytes 772
  123.5 204.4 %copy-start.39 = (f32[64]{0:T(128)}, f32[64]{0:T(128)S(1)}, u32[]{:S(2)}) copy-start(f32[64]{0:T(128)S(1)} %fusion.88) | copy-start | bytes 772
  123.5 204.4 %copy-start.29 = (f32[64]{0:T(128)}, f32[64]{0:T(128)S(1)}, u32[]{:S(2)}) copy-start(f32[64]{0:T(128)S(1)} %fusion.138) | copy-start | bytes 772
  124.7 367.8 %copy-start.21 = (pred[64,64]{0,1:T(8,128)(4,1)}, pred[64,64]{0,1:T(8,128)(4,1)S(1)}, u32[]{:S(2)}) copy-start(pred[64,64]{0,1:T(8,128)(4,1)S(1)} %get-tuple-element.20) | copy-start | bytes 12292
  184.7 308.1 %copy-start.13 = (bf16[64,8,64]{2,1,0:T(8,128)(2,1)}, bf16[64,8,64]{2,1,0:T(8,128)(2,1)S(1)}, u32[]{:S(2)}) copy-start(bf16[64,8,64]{2,1,0:T(8,128)(2,1)S(1)} %reshape.396) | copy-start | bytes 196612
  498.9 69.5 %all-to-all-start.2 = ((bf16[32,36,1024]{2,1,0:T(8,128)(2,1)}), bf16[32,36,1024]{2,1,0:T(8,128)(2,1)}, u32[]{:S(2)}, u32[]{:S(2)}) async-start(bf16[32,36,1024]{2,1,0:T(8,128)(2,1)} %bitcast.177), calls=%async_computation.2 | async-start | bytes 5242880 | tf_op jit(solution)/shard_map/all_to_all | solution.py:198
  568.5 77.7 %all-to-all-start.1 = ((bf16[32,36,1024]{2,1,0:T(8,128)(2,1)}), bf16[32,36,1024]{2,1,0:T(8,128)(2,1)}, u32[]{:S(2)}, u32[]{:S(2)}) async-start(bf16[32,36,1024]{2,1,0:T(8,128)(2,1)} %reshape.388), calls=%async_computation.1 | async-start | bytes 5242880 | tf_op jit(solution)/shard_map/all_to_all | solution.py:187
  646.2 220.3 %all-to-all-start.4 = ((bf16[32,36,1024]{2,1,0:T(8,128)(2,1)}), bf16[32,36,1024]{2,1,0:T(8,128)(2,1)}, u32[]{:S(2)}, u32[]{:S(2)}) async-start(bf16[32,36,1024]{2,1,0:T(8,128)(2,1)} %reshape.405), calls=%async_computation.4 | async-start | bytes 5242880 | tf_op jit(solution)/shard_map/all_to_all | solution.py:211
  655.5 204.2 %all-reduce.5.cloned.1.call-start = ((), (), s32[]{:S(2)}) async-start(), calls=%async_computation.8 | async-start | bytes 524288 | tf_op jit(solution)/shard_map/psum | solution.py:19
  672.9 188.5 %copy-start.15 = (bf16[64,8,64]{2,1,0:T(8,128)(2,1)S(1)}, bf16[64,8,64]{2,1,0:T(8,128)(2,1)}, u32[]{:S(2)}) copy-start(bf16[64,8,64]{2,1,0:T(8,128)(2,1)} %reshape.391) | copy-start | bytes 196612
  862.9 8.8 collective-permute-start
  869.7 13.7 %collective-permute-start.1 = (bf16[64,1024]{1,0:T(8,128)(2,1)S(1)}, bf16[64,1024]{1,0:T(8,128)(2,1)S(1)}, u32[]{:S(2)}, u32[]{:S(2)}) collective-permute-start(bf16[64,1024]{1,0:T(8,128)(2,1)S(1)} %add_convert_fusion), channel_id=1, source_target_pairs={{32,0},{64,32},{96,64},{128,96},{160,128},{192,160},{224,192},{256... | collective-permute-start | bytes 393224 | tf_op jit(solution)/shard_map/ppermute | solution.py:25
  (29 other events, 231.5 us)
Sparse Core Ops, SparseCore 0:
  10.1 172.8 all-gather.5
  185.0 142.7 all-gather.7
  330.0 160.1 all-gather.3
  670.3 189.3 all-reduce.4
where the time goes:
time: 894 us; the launch traced here: 892 us
  waiting for transfers between devices  714 us (80%)
  starting transfers between devices  71.4 us (8%)
  matrix products  38.9 us (4%)
  local copies, waits for them, and re-layouts  37.5 us (4%)
  other arithmetic  15.1 us (2%)
  between operations  14.8 us (2%)
    psum x1, waiting for transfers between devices, spread_2(): return lax.psum(jnp.where(mine, value, jnp.zeros_like(value)), axis)  187 us
    all_gather x1, waiting for transfers between devices, on_device(): lax.all_gather(w_keyval, 'expert', axis=1, tiled=True)  160 us
    all_gather x1, waiting for transfers between devices, on_device(): lax.all_gather(w_output, 'expert', axis=1, tiled=True)  143 us
    all_to_all x1, waiting for transfers between devices, on_device(): lax.all_to_all(send_a, 'expert', split_axis=0, concat_axis=0, tiled=True)  68.3 us
    all_gather x1, waiting for transfers between devices, on_device(): lax.all_gather(w_query, 'expert', axis=1, tiled=True)  58.2 us
    all_to_all x1, waiting for transfers between devices, on_device(): lax.all_to_all(send_d, 'expert', split_axis=0, concat_axis=0, tiled=True)  44.2 us
    all_to_all x1, waiting for transfers between devices, on_device(): lax.all_to_all(jnp.dot(units, down_slice, preferred_element_type=jnp.floa...  39.3 us
    all_to_all x1, starting transfers between devices, on_device(): lax.all_to_all(send_x, 'expert', split_axis=0, concat_axis=0, tiled=True)  18.2 us
  transfers between devices with their start and end apart: 11, of which 8 were waited for; matrix products, arithmetic and copies ran while one was open for 10% of the time, Pallas kernels for 0%

commit v1 on v0

v1 whole, which is shorter than its diff:
```python
import functools

import jax
import jax.numpy as jnp
from jax import lax
from jax.experimental import pallas as pl
from jax.experimental.pallas import tpu as pltpu
from jax.sharding import PartitionSpec as P

MESH = pl.DeviceIdType.MESH
HEAD_DIM = 64
EXPERTS = 4
SEQ = 32
NZ = 8
NY = 4
NSEC = 16
TOK = 64
LINE = NY * TOK
D = 1024
HALF = LINE // 2

EPS = 1e-05
ROOT_HALF = 0.7071067811865476
INV_ROOT_TWO_PI = 0.3989422804014327


def layer_norm(row_block, gain_row):
    values = row_block.astype(jnp.float32)
    center = values - jnp.mean(values, axis=-1, keepdims=True)
    spread = jnp.mean(center * center, axis=-1, keepdims=True)
    return center * lax.rsqrt(spread + EPS) * gain_row


def gelu_value(inputs):
    return 0.5 * inputs * (1.0 + lax.erf(inputs * ROOT_HALF))


def gelu_slope(inputs):
    return (
        0.5 * (1.0 + lax.erf(inputs * ROOT_HALF))
        + inputs * jnp.exp(-0.5 * inputs * inputs) * INV_ROOT_TWO_PI
    )


def row_lengths(sent_lens, row_count):
    sentence = jnp.arange(row_count) // SEQ
    sent_match = sentence[:, None] == jnp.arange(sent_lens.shape[0])[None, :]
    return jnp.sum(jnp.where(sent_match, sent_lens[None, :], 0), axis=1)


def cross_attend(middle, memory, src_len, gain_row, query_w, keyval_w, output_w):
    row_count = middle.shape[0]
    inner_width = query_w.shape[1]
    head_count = inner_width // HEAD_DIM
    normed = layer_norm(middle, gain_row).astype(jnp.bfloat16)
    query_rows = jnp.dot(normed, query_w, preferred_element_type=jnp.float32).astype(jnp.bfloat16)
    keyval = jnp.dot(memory, keyval_w, preferred_element_type=jnp.float32).astype(jnp.bfloat16)
    q_heads = query_rows.reshape(row_count, head_count, HEAD_DIM).astype(jnp.float32)
    k_heads = keyval[:, :inner_width].reshape(row_count, head_count, HEAD_DIM).astype(jnp.float32)
    v_heads = keyval[:, inner_width:].reshape(row_count, head_count, HEAD_DIM).astype(jnp.float32)
    scores = jnp.einsum("qhd,khd->hqk", q_heads, k_heads) * HEAD_DIM ** (-0.5)
    row_index = jnp.arange(row_count)
    sentence = row_index // SEQ
    key_len = row_lengths(src_len, row_count)
    allowed = (sentence[:, None] == sentence[None, :]) & (
        (row_index % SEQ)[None, :] < key_len[None, :]
    )
    raised = jnp.where(allowed[None], jnp.exp(scores), 0.0)
    weights = (raised / jnp.sum(raised, axis=-1, keepdims=True)).astype(jnp.bfloat16)
    mixed_heads = jnp.einsum("hqk,khd->qhd", weights.astype(jnp.float32), v_heads).astype(
        jnp.bfloat16
    )
    projected = jnp.dot(
        mixed_heads.reshape(row_count, inner_width), output_w, preferred_element_type=jnp.float32
    )
    return (middle.astype(jnp.float32) + projected).astype(jnp.bfloat16)


def place():
    me = lax.axis_index("expert")
    return me, lax.div(me, NY), lax.rem(me, NY)


def to_expert(z, y):
    return {"expert": lax.rem(z + 2 * NZ, NZ) * NY + lax.rem(y + 2 * NY, NY)}


def to_section(s):
    return {"section": lax.rem(s + 2 * NSEC, NSEC)}


def rows(ref, start, count):
    return ref.at[pl.ds(pl.multiple_of(start, 8), count)]


def remote(src, dst, send, recv, device):
    return pltpu.make_async_remote_copy(
        src_ref=src, dst_ref=dst, send_sem=send, recv_sem=recv, device_id=device, device_id_type=MESH
    )


def greet(devices):
    barrier = pltpu.get_barrier_semaphore()
    for device in devices:
        pl.semaphore_signal(barrier, inc=1, device_id=device, device_id_type=MESH)
    pl.semaphore_wait(barrier, len(devices))


def expert_neighbours():
    _, z, y = place()
    return [to_expert(z + 1, y), to_expert(z - 1, y)] + [to_expert(z, y + d) for d in (1, 2, 3)]


class Gather:
    def __init__(self, src, dst, local, ysend, yrecv, zsend, zrecv):
        self.src, self.dst, self.local = src, dst, local
        self.ysend, self.yrecv, self.zsend, self.zrecv = ysend, yrecv, zsend, zrecv
        self.size = src.shape[0]
        self.me, self.z, self.y = place()

    def own(self):
        return pltpu.make_async_copy(
            self.src, rows(self.dst, self.me * self.size, self.size), self.local
        )

    def line(self, d, arriving):
        index = self.z * NY + lax.rem(self.y + NY - d, NY) if arriving else self.me
        block = rows(self.dst, index * self.size, self.size)
        return remote(
            self.src, block, self.ysend.at[d - 1], self.yrecv.at[d - 1], to_expert(self.z, self.y + d)
        )

    def hop(self, way, step, arriving):
        sign = 1 if way == 0 else -1
        back = step + 1 if arriving else step
        origin = lax.rem(self.z - sign * back + 2 * NZ, NZ)
        start, count = origin * NY * self.size, NY * self.size
        if step == 3:
            count = count // 2
            start = start + way * count
        block = rows(self.dst, start, count)
        return remote(
            block, block, self.zsend.at[way, step], self.zrecv.at[way, step], to_expert(self.z + sign, self.y)
        )

    def begin(self):
        self.own().start()
        for d in (1, 2, 3):
            self.line(d, False).start()

    def step(self, s):
        if s == 0:
            self.own().wait()
            for d in (1, 2, 3):
                self.line(d, True).wait_recv()
        else:
            for way in (0, 1):
                self.hop(way, s - 1, True).wait_recv()
        for way in (0, 1):
            if s < 4:
                self.hop(way, s, False).start()

    def finish(self):
        for d in (1, 2, 3):
            self.line(d, False).wait_send()
        for way in (0, 1):
            for s in range(4):
                self.hop(way, s, False).wait_send()


GATHER_SEMS = [
    pltpu.SemaphoreType.DMA,
    pltpu.SemaphoreType.DMA((3,)),
    pltpu.SemaphoreType.DMA((3,)),
    pltpu.SemaphoreType.DMA((2, 4)),
    pltpu.SemaphoreType.DMA((2, 4)),
]


class Scatter:
    def __init__(self, src, slots, line_buf, line_slots, zsend, zrecv, ysend, yrecv):
        self.src, self.slots, self.line_buf, self.line_slots = src, slots, line_buf, line_slots
        self.zsend, self.zrecv, self.ysend, self.yrecv = zsend, zrecv, ysend, yrecv
        self.me, self.z, self.y = place()

    def mine(self, way, step, chunk):
        sign = 1 if way == 0 else -1
        dest = lax.rem(self.z + sign * (4 - step) + 2 * NZ, NZ)
        return pl.ds(pl.multiple_of(dest * LINE + chunk * HALF, HALF), HALF)

    def hop(self, way, step, chunk):
        sign = 1 if way == 0 else -1
        part = pl.ds(chunk * HALF, HALF)
        first = 0 if chunk == way else 1
        if step == first:
            source = self.src.at[self.mine(way, step, chunk)]
        else:
            source = self.slots.at[way, step - 1, part]
        return remote(
            source,
            self.slots.at[way, step, part],
            self.zsend.at[way, step, chunk],
            self.zrecv.at[way, step, chunk],
            to_expert(self.z + sign, self.y),
        )

    def step(self, s):
        for chunk in (0, 1):
            for way in (0, 1):
                first = 0 if chunk == way else 1
                part = pl.ds(chunk * HALF, HALF)
                if s < first:
                    continue
                if s > first:
                    self.hop(way, s - 1, chunk).wait_recv()
                    if s < 4:
                        self.slots[way, s - 1, part] = (
                            self.slots[way, s - 1, part].astype(jnp.float32)
                            + self.src[self.mine(way, s, chunk)].astype(jnp.float32)
                        ).astype(jnp.bfloat16)
                if s < 4:
                    self.hop(way, s, chunk).start()

    def line(self, d):
        target = lax.rem(self.y + d, NY)
        return remote(
            rows(self.line_buf, target * TOK, TOK),
            self.line_slots.at[d - 1],
            self.ysend.at[d - 1],
            self.yrecv.at[d - 1],
            to_expert(self.z, self.y + d),
        )

    def cross(self):
        for chunk in (0, 1):
            part = pl.ds(chunk * HALF, HALF)
            own = self.src[pl.ds(pl.multiple_of(self.z * LINE + chunk * HALF, HALF), HALF)]
            self.line_buf[part] = (
                own.astype(jnp.float32)
                + self.slots[0, 3, part].astype(jnp.float32)
                + self.slots[1, 3, part].astype(jnp.float32)
            ).astype(jnp.bfloat16)
        for d in (1, 2, 3):
            self.line(d).start()

    def total(self):
        for d in (1, 2, 3):
            self.line(d).wait_recv()
        result = self.line_buf[pl.ds(pl.multiple_of(self.y * TOK, TOK), TOK)].astype(jnp.float32)
        for d in (1, 2, 3):
            result = result + self.line_slots[d - 1].astype(jnp.float32)
        return result

    def finish(self):
        for chunk in (0, 1):
            for way in (0, 1):
                for s in range(0 if chunk == way else 1, 4):
                    self.hop(way, s, chunk).wait_send()
        for d in (1, 2, 3):
            self.line(d).wait_send()


SCATTER_SCRATCH = [
    pltpu.VMEM((2, 4, LINE, D), jnp.bfloat16),
    pltpu.VMEM((LINE, D), jnp.bfloat16),
    pltpu.VMEM((3, TOK, D), jnp.bfloat16),
    pltpu.SemaphoreType.DMA((2, 4, 2)),
    pltpu.SemaphoreType.DMA((2, 4, 2)),
    pltpu.SemaphoreType.DMA((3,)),
    pltpu.SemaphoreType.DMA((3,)),
]


def gather_kernel(count, *refs):
    srcs, dsts, sems = refs[:count], refs[count : 2 * count], refs[2 * count :]
    gathers = [Gather(srcs[i], dsts[i], *sems[5 * i : 5 * i + 5]) for i in range(count)]
    greet(expert_neighbours())
    for g in gathers:
        g.begin()
    for s in range(5):
        for g in gathers:
            g.step(s)
    for g in gathers:
        g.finish()


def all_gathered(arrays):
    count = len(arrays)
    return pl.pallas_call(
        functools.partial(gather_kernel, count),
        out_shape=[
            jax.ShapeDtypeStruct((NZ * NY * a.shape[0],) + a.shape[1:], a.dtype) for a in arrays
        ],
        in_specs=[pl.BlockSpec(memory_space=pl.ANY)] * count,
        out_specs=[pl.BlockSpec(memory_space=pl.ANY)] * count,
        scratch_shapes=GATHER_SEMS * count,
        compiler_params=pltpu.CompilerParams(
            collective_id=0, has_side_effects=True, vmem_limit_bytes=48 * 2**20
        ),
        name="gather_rows_weights",
    )(*arrays)


def scatter_gather_kernel(part_ref, grad_ref, total_ref, gathered_ref, *scratch):
    scatter = Scatter(part_ref, *scratch[:7])
    gather = Gather(grad_ref, gathered_ref, *scratch[7:])
    greet(expert_neighbours())
    gather.begin()
    for s in range(5):
        scatter.step(s)
        gather.step(s)
    scatter.cross()
    total_ref[...] = scatter.total()
    gather.finish()
    scatter.finish()


def scatter_and_gather(partial_rows, grad_rows):
    return pl.pallas_call(
        scatter_gather_kernel,
        out_shape=[
            jax.ShapeDtypeStruct((TOK, D), jnp.float32),
            jax.ShapeDtypeStruct((NZ * NY * TOK, D), jnp.bfloat16),
        ],
        in_specs=[pl.BlockSpec(memory_space=pltpu.VMEM), pl.BlockSpec(memory_space=pl.ANY)],
        out_specs=[pl.BlockSpec(memory_space=pltpu.VMEM), pl.BlockSpec(memory_space=pl.ANY)],
        scratch_shapes=SCATTER_SCRATCH + GATHER_SEMS,
        compiler_params=pltpu.CompilerParams(
            collective_id=1, has_side_effects=True, vmem_limit_bytes=48 * 2**20
        ),
        name="scatter_outputs_gather_grads",
    )(partial_rows, grad_rows)


PIECE_ROWS = 32
PIECE_COLS = 128


def piece(ref, index):
    row = pl.multiple_of(lax.div(index, 8) * PIECE_ROWS, PIECE_ROWS)
    col = pl.multiple_of(lax.rem(index, 8) * PIECE_COLS, PIECE_COLS)
    return ref.at[pl.ds(row, PIECE_ROWS), pl.ds(col, PIECE_COLS)]


def scatter_section_kernel(root, *refs):
    (part_ref, mid_ref, term_ref, total_ref, memory_ref, grad_ref, mem_buf, terms, grad_buf) = refs[:9]
    (bsend, brecv, tsend, trecv, gsend, grecv) = refs[9:15]
    scatter = Scatter(part_ref, *refs[15:])
    s = lax.axis_index("section")
    greet(expert_neighbours() + [to_section(s + d) for d in range(1, NSEC)])

    def spread(slot, target):
        return remote(mem_buf, mem_buf, bsend.at[slot], brecv, to_section(target))

    is_root = s == root
    is_leader = lax.rem(s, 4) == root % 4

    @pl.when(is_root)
    def _():
        mem_buf[...] = mid_ref[...]
        for slot in (0, 1, 2):
            spread(slot, s + 4 * (slot + 1)).start()

    def term(d):
        target = lax.rem(s + d, NSEC)
        return remote(piece(term_ref, target), terms.at[d - 1], tsend.at[d - 1], trecv.at[d - 1], to_section(s + d))

    for d in range(1, NSEC):
        term(d).start()
    scatter.step(0)
    scatter.step(1)

    @pl.when(jnp.logical_not(is_root))
    def _():
        spread(0, s + 1).wait_recv()

    @pl.when(is_leader)
    def _():
        for slot, d in ((3, 1), (4, -1), (5, -2)):
            spread(slot, s + d).start()

    for d in range(1, NSEC):
        term(d).wait_recv()
    own = piece(term_ref, s)[...].astype(jnp.float32)
    for d in range(1, NSEC):
        own = own + terms[d - 1].astype(jnp.float32)
    own_view = piece(grad_buf, s)
    own_view[...] = own.astype(jnp.bfloat16)

    def result(d, arriving):
        index = lax.rem(s + NSEC - d, NSEC) if arriving else s
        view = piece(grad_buf, index)
        return remote(view, view, gsend.at[d - 1], grecv.at[d - 1], to_section(s + d))

    for d in range(1, NSEC):
        result(d, False).start()
    scatter.step(2)
    scatter.step(3)
    scatter.step(4)
    scatter.cross()
    for d in range(1, NSEC):
        result(d, True).wait_recv()
    grad_ref[...] = grad_buf[...]
    memory_ref[...] = mem_buf[...]
    total_ref[...] = scatter.total()
    for d in range(1, NSEC):
        term(d).wait_send()
        result(d, False).wait_send()

    @pl.when(is_root)
    def _():
        for slot in (0, 1, 2):
            spread(slot, s + 4).wait_send()

    @pl.when(is_leader)
    def _():
        for slot in (3, 4, 5):
            spread(slot, s + 1).wait_send()

    scatter.finish()


def scatter_and_sections(root, partial_rows, middle, memory_term):
    return pl.pallas_call(
        functools.partial(scatter_section_kernel, root),
        out_shape=[
            jax.ShapeDtypeStruct((TOK, D), jnp.float32),
            jax.ShapeDtypeStruct((TOK, D), jnp.bfloat16),
            jax.ShapeDtypeStruct((TOK, D), jnp.bfloat16),
        ],
        in_specs=[pl.BlockSpec(memory_space=pltpu.VMEM)] * 3,
        out_specs=[pl.BlockSpec(memory_space=pltpu.VMEM)] * 3,
        scratch_shapes=[
            pltpu.VMEM((TOK, D), jnp.bfloat16),
            pltpu.VMEM((NSEC - 1, PIECE_ROWS, PIECE_COLS), jnp.bfloat16),
            pltpu.VMEM((TOK, D), jnp.bfloat16),
            pltpu.SemaphoreType.DMA((6,)),
            pltpu.SemaphoreType.DMA,
            pltpu.SemaphoreType.DMA((NSEC - 1,)),
            pltpu.SemaphoreType.DMA((NSEC - 1,)),
            pltpu.SemaphoreType.DMA((NSEC - 1,)),
            pltpu.SemaphoreType.DMA((NSEC - 1,)),
        ]
        + SCATTER_SCRATCH,
        compiler_params=pltpu.CompilerParams(
            collective_id=2, has_side_effects=True, vmem_limit_bytes=48 * 2**20
        ),
        name="scatter_grads_spread_memory",
    )(partial_rows, middle, memory_term)


def pass_kernel(rows_ref, grads_ref, rows_out, grads_out, rows_slot, grads_slot, send, recv):
    s = lax.axis_index("section")
    ahead, behind = to_section(s + 1), to_section(s - 1)
    greet([ahead, behind])
    forward = remote(rows_ref, rows_slot, send.at[0], recv.at[0], ahead)
    backward = remote(grads_ref, grads_slot, send.at[1], recv.at[1], behind)
    forward.start()
    backward.start()
    forward.wait_recv()
    rows_out[...] = rows_slot[...]
    backward.wait_recv()
    grads_out[...] = grads_slot[...]
    forward.wait_send()
    backward.wait_send()


def passed(out_rows, grad_rows):
    shape = jax.ShapeDtypeStruct((TOK, D), jnp.bfloat16)
    return pl.pallas_call(
        pass_kernel,
        out_shape=[shape, shape],
        in_specs=[pl.BlockSpec(memory_space=pltpu.VMEM)] * 2,
        out_specs=[pl.BlockSpec(memory_space=pltpu.VMEM)] * 2,
        scratch_shapes=[
            pltpu.VMEM((TOK, D), jnp.bfloat16),
            pltpu.VMEM((TOK, D), jnp.bfloat16),
            pltpu.SemaphoreType.DMA((2,)),
            pltpu.SemaphoreType.DMA((2,)),
        ],
        compiler_params=pltpu.CompilerParams(collective_id=3, has_side_effects=True),
        name="pass_rows_grads",
    )(out_rows, grad_rows)


def expert_shares(routes, probs, live):
    named = routes[:, :, None] == jnp.arange(EXPERTS)[None, None, :]
    return jnp.sum(jnp.where(named, probs[:, :, None], 0.0), axis=1) * live[:, None]


def on_device(
    hidden_fwd,
    hidden_bwd,
    mid_bwd,
    grads_in,
    memory_saved,
    lengths,
    routes_fwd,
    routes_bwd,
    probs_fwd,
    probs_bwd,
    norm_gains,
    w_in,
    w_out,
    w_query,
    w_keyval,
    w_output,
):
    first_decoder = 3
    is_decoder = lax.axis_index("section") >= first_decoder
    my_expert = lax.axis_index("expert") // 8
    gain_moe = norm_gains[0, 0]
    gain_att = norm_gains[0, 1]
    up_slice = w_in[0]
    down_slice = w_out[0]
    position = jnp.arange(TOK) % SEQ
    lens_fwd = jnp.where(is_decoder, lengths[1], lengths[0])
    lens_bwd = jnp.where(is_decoder, lengths[3], lengths[2])
    live_fwd = (position < row_lengths(lens_fwd, TOK)).astype(jnp.float32)
    live_bwd = (position < row_lengths(lens_bwd, TOK)).astype(jnp.float32)
    hidden_a = hidden_fwd[0]
    hidden_b = hidden_bwd[0]
    normed_a = layer_norm(hidden_a, gain_moe).astype(jnp.bfloat16)
    normed_b = layer_norm(hidden_b, gain_moe).astype(jnp.bfloat16)
    shares = jnp.concatenate(
        [
            expert_shares(routes_fwd[0], probs_fwd[0], live_fwd).T,
            expert_shares(routes_bwd[0], probs_bwd[0], live_bwd).T,
        ],
        axis=1,
    )
    shares = jnp.concatenate([shares, jnp.zeros_like(shares)], axis=0)
    all_a, all_b, keyval_w, query_w, output_w, all_shares = all_gathered(
        [normed_a, normed_b, w_keyval[0], w_query[0], w_output[0], shares]
    )
    all_shares = lax.dynamic_index_in_dim(
        all_shares.reshape(NZ * NY, 8, 2 * TOK), my_expert, axis=1, keepdims=False
    )
    share_a = all_shares[:, :TOK].reshape(-1, 1)
    share_b = all_shares[:, TOK:].reshape(-1, 1)
    cotangent = grads_in[0]

    def attend_saved(mid_rows, mem_rows):
        return cross_attend(mid_rows, mem_rows, lengths[2], gain_att, query_w, keyval_w, output_w)

    _, attend_grad = jax.vjp(attend_saved, mid_bwd[0], memory_saved)
    grad_mid, grad_memory = attend_grad(cotangent)
    upstream = jnp.where(is_decoder, grad_mid, cotangent)
    memory_term = jnp.where(is_decoder, grad_memory, jnp.zeros_like(grad_memory))

    units = gelu_value(jnp.dot(all_a, up_slice, preferred_element_type=jnp.float32)).astype(
        jnp.bfloat16
    )
    part_a = (jnp.dot(units, down_slice, preferred_element_type=jnp.float32) * share_a).astype(
        jnp.bfloat16
    )
    mixed_a, all_grads = scatter_and_gather(part_a, upstream)
    middle_a = (hidden_a.astype(jnp.float32) + mixed_a).astype(jnp.bfloat16)

    sent_rows = (all_grads.astype(jnp.float32) * share_b).astype(jnp.bfloat16)
    pre_act = jnp.dot(all_b, up_slice, preferred_element_type=jnp.float32)
    through = lax.dot_general(
        sent_rows, down_slice, (((1,), (1,)), ((), ())), preferred_element_type=jnp.float32
    )
    unit_grad = (through * gelu_slope(pre_act)).astype(jnp.bfloat16)
    part_b = lax.dot_general(
        unit_grad, up_slice, (((1,), (1,)), ((), ())), preferred_element_type=jnp.float32
    ).astype(jnp.bfloat16)
    grad_units, memory, memory_grad = scatter_and_sections(
        first_decoder - 1, part_b, middle_a, memory_term
    )
    attended = cross_attend(middle_a, memory, lengths[0], gain_att, query_w, keyval_w, output_w)
    out_a = jnp.where(is_decoder, attended, middle_a)

    def norm_only(inputs):
        return layer_norm(inputs, gain_moe)

    _, norm_grad = jax.vjp(norm_only, hidden_b.astype(jnp.float32))
    grad_hidden = (upstream.astype(jnp.float32) + norm_grad(grad_units)[0]).astype(jnp.bfloat16)
    passed_rows, passed_grads = passed(out_a, grad_hidden)
    return (passed_rows[None], passed_grads[None], memory_grad)


def solution(mesh):
    return jax.shard_map(
        on_device,
        mesh=mesh,
        in_specs=(
            P("section", "expert", None),
            P("section", "expert", None),
            P("section", "expert", None),
            P("section", "expert", None),
            P("expert", None),
            P(None, "expert"),
            P("section", "expert", None),
            P("section", "expert", None),
            P("section", "expert", None),
            P("section", "expert", None),
            P("section", None, None),
            P("section", None, "expert"),
            P("section", "expert", None),
            P("section", "expert", None),
            P("section", "expert", None),
            P("section", "expert", None),
        ),
        out_specs=(P("section", "expert", None), P("section", "expert", None), P("expert", None)),
        check_vma=False,
    )
```

time: 894 us -> 414 us (0.46)
  the two profiles are of different devices: /device:TPU:55 before, /device:TPU:72 now
where the time goes in v1:
time: 414 us; the launch traced here: 413 us
  Pallas kernels  333 us (80%)
  matrix products  40.1 us (10%)
  local copies, waits for them, and re-layouts  22.7 us (5%)
  other arithmetic  16.4 us (4%)
    pallas_call x1, Pallas kernels, all_gathered(): pl.pallas_call(functools.partial(gather_kernel, count), out_shape=[jax.Sh...  149 us
    pallas_call x1, Pallas kernels, scatter_and_gather(): pl.pallas_call(scatter_gather_kernel, out_shape=[jax.ShapeDtypeStruct((TO...  101 us
    pallas_call x1, Pallas kernels, scatter_and_sections(): pl.pallas_call(functools.partial(scatter_section_kernel, root), out_shape...  67.1 us
    pallas_call x1, Pallas kernels, passed(): pl.pallas_call(pass_kernel, out_shape=[shape, shape], in_specs=[pl.BlockS...  15.6 us
    unnamed x63, local copies, waits for them, and re-layouts  13.1 us
    dot_general x1, matrix products, on_device(): lax.dot_general(unit_grad, up_slice, (((1,), (1,)), ((), ())), preferred_...  9.63 us

profile of v1, /device:TPU:72, one launch (start us, length us, event | category | flops | bytes accessed | tf_op | source)
XLA Modules:
  0.0 413.1 jit_solution(15314094343078570423)
XLA Ops:
  11.5 1.2 fusion.56
  15.0 149.2 %gather_rows_weights.1 = (bf16[2048,1024]{1,0:T(8,128)(2,1)}, bf16[2048,1024]{1,0:T(8,128)(2,1)}, bf16[1024,1024]{1,0:T(8,128)(2,1)S(1)}, bf16[1024,512]{1,0:T(8...) custom-call(bf16[64,1024]{1,0:T(8,128)(2,1)S(1)} %get-tuple-element.48.refs_0_, ...), custom_call_target="tpu_custom_call" | custom-call | tf_op jit(solution)/shard_map/gather_rows_weights/pallas_call | solution.py:289
  167.1 8.1 %multiply_convert_fusion.1.part_ref = bf16[2048,1024]{1,0:T(8,128)(2,1)} fusion(f32[2048]{0:T(1024)S(1)} %mul.269, bf16[1,512,1024]{2,1,0:T(8,128)(2,1)} %param.28, bf16[2048,1024]{1,0:T(8,128)(2,1)} %get-tuple-element.16, bf16[1,1024,512]{2,1,0:T(8,128)(2,1)S(1)} %copy-done), kind=kOutput, calls=%fused_computation.1 | convolution fusion | flops 4304404480 | bytes 10493952 | tf_op jit(solution)/shard_map/dot_general | solution.py:554
  175.2 6.6 %fusion.28 = f32[2048,512]{1,0:T(8,128)} fusion(bf16[2048,1024]{1,0:T(8,128)(2,1)} %get-tuple-element.23, bf16[1,1024,512]{2,1,0:T(8,128)(2,1)S(1)} %copy-done), kind=kOutput, calls=%fused_computation.47 | convolution fusion | flops 2147483648 | bytes 9437184 | tf_op jit(solution)/shard_map/dot_general | solution.py:561
  182.3 1.6 convolution_convert_fusion.11
  184.7 1.4 fusion.20
  187.7 1.6 reshape.290
  189.4 1.2 select_reduce_fusion
  192.1 1.6 copy.62
  193.7 1.1 multiply_reduce_fusion
  194.9 1.2 fusion.19
  196.1 1.2 fusion.18
  199.1 1.6 fusion.22.refs_2_
  200.7 1.8 fusion.66
  204.5 100.9 %scatter_outputs_gather_grads.1 = (f32[64,1024]{1,0:T(8,128)S(1)}, bf16[2048,1024]{1,0:T(8,128)(2,1)S(1)}) custom-call(bf16[2048,1024]{1,0:T(8,128)(2,1)} %multiply_convert_fusion.1.part_ref, bf16[64,1024]{1,0:T(8,128)(2,1)S(1)} %add_select_fusion.grad_ref), custom_call_target="tpu_custom_call" | custom-call | tf_op jit(solution)/shard_map/scatter_outputs_gather_grads/pallas_call | solution.py:319
  306.1 2.0 copy-done.12
  308.1 9.6 %convolution_convert_fusion.refs_0_ = bf16[2048,1024]{1,0:T(8,128)(2,1)} fusion(f32[2048,512]{1,0:T(8,128)} %fusion.28, bf16[2048,1024]{1,0:T(8,128)(2,1)} %copy-done.12, f32[2048]{0:T(1024)} %mul.291, bf16[1,512,1024]{2,1,0:T(8,128)(2,1)} %param.28, bf16[1,1024,512]{2,1,0:T(8,128)(2,1)S(1)} %copy-done), kind=kOutput, calls=%fused_computation.12 | convolution fusion | flops 4313841664 | bytes 14688256 | tf_op jit(solution)/shard_map/dot_general | solution.py:566
  317.7 1.2 convert_reduce_fusion
  318.9 2.2 copy-done.3
  321.1 67.1 %scatter_grads_spread_memory.1 = (f32[64,1024]{1,0:T(8,128)S(1)}, bf16[64,1024]{1,0:T(8,128)(2,1)S(1)}, bf16[64,1024]{1,0:T(8,128)(2,1)S(1)}) custom-call(bf16[2048,1024]{1,0:T(8,128)(2,1)S(1)} %copy-done.3, bf16[64,1024]{1,0:T(8,128)(2,1)S(1)} %get-tuple-element.38.refs_1_, bf16[64,1024]{1,0:T(8,128)(2,1)S(1)} %fusion.22.refs_2_), custom_call_target="tpu_custom_call" | custom-call | tf_op jit(solution)/shard_map/scatter_grads_spread_memory/pallas_call | solution.py:424
  391.5 2.2 fusion.21.rows_ref
  393.7 15.6 %pass_rows_grads.1 = (bf16[64,1024]{1,0:T(8,128)(2,1)}, bf16[64,1024]{1,0:T(8,128)(2,1)}) custom-call(bf16[64,1024]{1,0:T(8,128)(2,1)} %fusion.21.rows_ref, bf16[64,1024]{1,0:T(8,128)(2,1)} %add_convert_fusion.grads_ref), custom_call_target="tpu_custom_call" | custom-call | tf_op jit(solution)/shard_map/pass_rows_grads/pallas_call | solution.py:470
  409.3 1.6 copy.97
  410.9 1.6 copy.98
  (118 shorter events, 28.6 us)
Async XLA Ops:
  0.6 166.5 %copy-start = (bf16[1,1024,512]{2,1,0:T(8,128)(2,1)S(1)}, bf16[1,1024,512]{2,1,0:T(8,128)(2,1)}, u32[]{:S(2)}) copy-start(bf16[1,1024,512]{2,1,0:T(8,128)(2,1)} %param.27) | copy-start | bytes 3145732
  4.0 8.7 %copy-start.17 = (f32[64]{0:T(128)}, f32[64]{0:T(128)S(1)}, u32[]{:S(2)}) copy-start(f32[64]{0:T(128)S(1)} %get-tuple-element.58) | copy-start | bytes 772
  5.1 1.1 copy-start.27
  5.1 161.2 %copy-start.22 = (f32[64]{0:T(128)}, f32[64]{0:T(128)S(1)}, u32[]{:S(2)}) copy-start(f32[64]{0:T(128)S(1)} %fusion.93) | copy-start | bytes 772
  6.2 176.1 %copy-start.19 = (f32[64]{0:T(128)}, f32[64]{0:T(128)S(1)}, u32[]{:S(2)}) copy-start(f32[64]{0:T(128)S(1)} %broadcast_multiply_fusion.1) | copy-start | bytes 772
  7.3 2.6 copy-start.29
  7.3 175.0 %copy-start.24 = (f32[64]{0:T(128)}, f32[64]{0:T(128)S(1)}, u32[]{:S(2)}) copy-start(f32[64]{0:T(128)S(1)} %fusion.94) | copy-start | bytes 772
  165.2 1.1 copy-start.4
  175.1 6.6 %copy-start.5 = (bf16[512,1024]{1,0:T(8,128)(2,1)S(1)}, bf16[512,1024]{1,0:T(8,128)(2,1)}, u32[]{:S(2)}) copy-start(bf16[512,1024]{1,0:T(8,128)(2,1)} %copy-done.4) | copy-start | bytes 3145732
  175.1 6.6 %copy-start.15 = (bf16[1,64,1024]{2,1,0:T(8,128)(2,1)S(1)}, bf16[1,64,1024]{2,1,0:T(8,128)(2,1)}, u32[]{:S(2)}) copy-start(bf16[1,64,1024]{2,1,0:T(8,128)(2,1)} %param.19) | copy-start | bytes 393220
  175.2 7.2 %copy-start.14 = (bf16[1,64,1024]{2,1,0:T(8,128)(2,1)S(1)}, bf16[1,64,1024]{2,1,0:T(8,128)(2,1)}, u32[]{:S(2)}) copy-start(bf16[1,64,1024]{2,1,0:T(8,128)(2,1)} %param.18) | copy-start | bytes 393220
  190.6 1.6 copy-start.26
  197.3 5.9 %copy-start.20 = (f32[64]{0:T(128)S(1)}, f32[64]{0:T(128)}, u32[]{:S(2)}) copy-start(f32[64]{0:T(128)} %copy-done.19) | copy-start | bytes 772
  197.3 5.9 %copy-start.25 = (f32[64]{0:T(128)S(1)}, f32[64]{0:T(128)}, u32[]{:S(2)}) copy-start(f32[64]{0:T(128)} %copy-done.24) | copy-start | bytes 772
  306.1 2.0 copy-start.12
  317.7 71.3 %copy-start.2 = (bf16[1024,512]{1,0:T(8,128)(2,1)S(1)}, bf16[1024,512]{1,0:T(8,128)(2,1)}, u32[]{:S(2)}) copy-start(bf16[1024,512]{1,0:T(8,128)(2,1)} %copy-done.1) | copy-start | bytes 3145732
  318.9 2.2 copy-start.3
  321.1 68.3 %copy-start.13 = (bf16[1,64,1024]{2,1,0:T(8,128)(2,1)S(1)}, bf16[1,64,1024]{2,1,0:T(8,128)(2,1)}, u32[]{:S(2)}) copy-start(bf16[1,64,1024]{2,1,0:T(8,128)(2,1)} %param.17) | copy-start | bytes 393220
  321.1 68.3 %copy-start.18 = (f32[64]{0:T(128)S(1)}, f32[64]{0:T(128)}, u32[]{:S(2)}) copy-start(f32[64]{0:T(128)} %copy-done.17) | copy-start | bytes 772
  321.1 68.5 %copy-start.28 = (f32[64]{0:T(128)S(1)}, f32[64]{0:T(128)}, u32[]{:S(2)}) copy-start(f32[64]{0:T(128)} %copy-done.27) | copy-start | bytes 772
  321.1 68.5 %copy-start.23 = (f32[64]{0:T(128)S(1)}, f32[64]{0:T(128)}, u32[]{:S(2)}) copy-start(f32[64]{0:T(128)} %copy-done.22) | copy-start | bytes 772
  321.1 69.8 %copy-start.21 = (pred[64,64]{0,1:T(8,128)(4,1)S(1)}, pred[64,64]{0,1:T(8,128)(4,1)}, u32[]{:S(2)}) copy-start(pred[64,64]{0,1:T(8,128)(4,1)} %get-tuple-element.49) | copy-start | bytes 12292
  388.3 1.1 copy-start.7
  389.6 22.9 %copy-start.8 = (bf16[64,1024]{1,0:T(8,128)(2,1)S(1)}, bf16[64,1024]{1,0:T(8,128)(2,1)}, u32[]{:S(2)}) copy-start(bf16[64,1024]{1,0:T(8,128)(2,1)} %copy-done.7) | copy-start | bytes 393220
  (6 other events, 4.7 us)

commit v2 on v0

v2 whole, which is shorter than its diff:
```python
import functools

import jax
import jax.numpy as jnp
from jax import lax
from jax.experimental import pallas as pl
from jax.experimental.pallas import tpu as pltpu
from jax.sharding import PartitionSpec as P

MESH = pl.DeviceIdType.MESH
BF16 = jnp.bfloat16
F32 = jnp.float32
HEAD_DIM = 64
EXPERTS = 4
SEQ = 32
NZ = 8
NY = 4
NSEC = 16
FIRST_DECODER = 3
ROOT = FIRST_DECODER - 1
TOK = 64
LINE = NY * TOK
HALF = LINE // 2
ROWS = NZ * LINE
D = 1024
UNITS = 512
INNER = 512
PAIR = 2 * HEAD_DIM

EPS = 1e-05
ROOT_HALF = 0.7071067811865476
INV_ROOT_TWO_PI = 0.3989422804014327


def dot_nn(a, b):
    return lax.dot_general(a, b, (((1,), (0,)), ((), ())), preferred_element_type=F32)


def dot_nt(a, b):
    return lax.dot_general(a, b, (((1,), (1,)), ((), ())), preferred_element_type=F32)


def dot_tn(a, b):
    return lax.dot_general(a, b, (((0,), (0,)), ((), ())), preferred_element_type=F32)


def norm_parts(row_block):
    values = row_block.astype(F32)
    center = values - jnp.mean(values, axis=-1, keepdims=True)
    spread = jnp.mean(center * center, axis=-1, keepdims=True)
    scale = lax.rsqrt(spread + EPS)
    return center * scale, scale


def norm_rows(row_block, gain_row):
    return (norm_parts(row_block)[0] * gain_row).astype(BF16)


def norm_grad(row_block, gain_row, upstream):
    unit, scale = norm_parts(row_block)
    grad = upstream * gain_row
    mean_grad = jnp.mean(grad, axis=-1, keepdims=True)
    mean_along = jnp.mean(grad * unit, axis=-1, keepdims=True)
    return scale * (grad - mean_grad - unit * mean_along)


def gelu_value(inputs):
    return 0.5 * inputs * (1.0 + lax.erf(inputs * ROOT_HALF))


def gelu_slope(inputs):
    return (
        0.5 * (1.0 + lax.erf(inputs * ROOT_HALF))
        + inputs * jnp.exp(-0.5 * inputs * inputs) * INV_ROOT_TWO_PI
    )


def allowed_keys(len_first, len_second):
    row = lax.broadcasted_iota(jnp.int32, (TOK, TOK), 0)
    col = lax.broadcasted_iota(jnp.int32, (TOK, TOK), 1)
    col_len = jnp.where(col < SEQ, len_first, len_second)
    same = (row < SEQ) == (col < SEQ)
    return same & (jnp.where(col < SEQ, col, col - SEQ) < col_len)


def live_column(len_first, len_second):
    row = lax.broadcasted_iota(jnp.int32, (TOK, 1), 0)
    row_len = jnp.where(row < SEQ, len_first, len_second)
    return jnp.where(jnp.where(row < SEQ, row, row - SEQ) < row_len, 1.0, 0.0)


def one_head(values, side):
    lane = lax.broadcasted_iota(jnp.int32, values.shape, 1)
    return jnp.where((lane < HEAD_DIM) == (side == 0), values, jnp.zeros_like(values))


def head_weights(query, key, allowed):
    scores = dot_nt(query, key) * HEAD_DIM ** (-0.5)
    raised = jnp.where(allowed, jnp.exp(scores), 0.0)
    return raised / jnp.sum(raised, axis=-1, keepdims=True)


def mix_pair(query, key, value, allowed):
    mixed = jnp.zeros((TOK, PAIR), F32)
    for side in (0, 1):
        weights = head_weights(one_head(query, side), key, allowed).astype(BF16)
        mixed = mixed + dot_nn(weights, one_head(value, side))
    return mixed.astype(BF16)


def mix_pair_grad(query, key, value, d_mixed, allowed):
    d_query = jnp.zeros((TOK, PAIR), F32)
    d_key = jnp.zeros((TOK, PAIR), F32)
    d_value = jnp.zeros((TOK, PAIR), F32)
    for side in (0, 1):
        query_one, grad_one = one_head(query, side), one_head(d_mixed, side)
        exact = head_weights(query_one, key, allowed)
        d_weights = dot_nt(grad_one, value).astype(BF16).astype(F32)
        d_value = d_value + dot_tn(exact.astype(BF16), grad_one)
        along = jnp.sum(d_weights * exact, axis=-1, keepdims=True)
        d_scores = (exact * (d_weights - along) * HEAD_DIM ** (-0.5)).astype(BF16)
        d_query = d_query + dot_nn(d_scores, one_head(key, side))
        d_key = d_key + dot_tn(d_scores, query_one)
    return d_query.astype(BF16), d_key.astype(BF16), d_value.astype(BF16)


def turned(column):
    eye = lax.broadcasted_iota(jnp.int32, (TOK, TOK), 0) == lax.broadcasted_iota(
        jnp.int32, (TOK, TOK), 1
    )
    return jnp.sum(jnp.where(eye, column, 0.0), axis=0, keepdims=True)


def upright(row):
    eye = lax.broadcasted_iota(jnp.int32, (TOK, TOK), 0) == lax.broadcasted_iota(
        jnp.int32, (TOK, TOK), 1
    )
    return jnp.sum(jnp.where(eye, row, 0.0), axis=1, keepdims=True)


def place():
    me = lax.axis_index("expert")
    return me, lax.div(me, NY), lax.rem(me, NY)


def to_expert(z, y):
    return {"expert": lax.rem(z + 2 * NZ, NZ) * NY + lax.rem(y + 2 * NY, NY)}


def to_section(s):
    return {"section": lax.rem(s + 2 * NSEC, NSEC)}


def remote(src, dst, send, recv, device):
    return pltpu.make_async_remote_copy(
        src_ref=src, dst_ref=dst, send_sem=send, recv_sem=recv, device_id=device, device_id_type=MESH
    )


class Gather:
    def __init__(self, array, size, first_col, cols, ysend, yrecv, zsend, zrecv):
        self.array, self.size, self.cols = array, size, pl.ds(first_col, cols)
        self.ysend, self.yrecv, self.zsend, self.zrecv = ysend, yrecv, zsend, zrecv
        self.me, self.z, self.y = place()

    def block(self, start, count):
        return self.array.at[pl.ds(pl.multiple_of(start, 8), count), self.cols]

    def line(self, d, arriving):
        index = self.z * NY + lax.rem(self.y + NY - d, NY) if arriving else self.me
        block = self.block(index * self.size, self.size)
        return remote(
            block, block, self.ysend.at[d - 1], self.yrecv.at[d - 1], to_expert(self.z, self.y + d)
        )

    def hop(self, way, step, arriving):
        sign = 1 if way == 0 else -1
        back = step + 1 if arriving else step
        origin = lax.rem(self.z - sign * back + 2 * NZ, NZ)
        start, count = origin * NY * self.size, NY * self.size
        if step == 3:
            count = count // 2
            start = start + way * count
        block = self.block(start, count)
        return remote(
            block,
            block,
            self.zsend.at[way, step],
            self.zrecv.at[way, step],
            to_expert(self.z + sign, self.y),
        )

    def begin(self):
        for d in (1, 2, 3):
            self.line(d, False).start()

    def step(self, s):
        if s == 0:
            for d in (1, 2, 3):
                self.line(d, True).wait_recv()
        for way in (0, 1):
            if s > 0:
                self.hop(way, s - 1, True).wait_recv()
            if s < 4:
                self.hop(way, s, False).start()

    def finish(self):
        for d in (1, 2, 3):
            self.line(d, False).wait_send()
        for way in (0, 1):
            for s in range(4):
                self.hop(way, s, False).wait_send()


GATHER_SEMS = [
    pltpu.SemaphoreType.DMA((3,)),
    pltpu.SemaphoreType.DMA((3,)),
    pltpu.SemaphoreType.DMA((2, 4)),
    pltpu.SemaphoreType.DMA((2, 4)),
]


class Scatter:
    def __init__(self, src, slots, line_buf, line_slots, zsend, zrecv, ysend, yrecv):
        self.src, self.slots, self.line_buf, self.line_slots = src, slots, line_buf, line_slots
        self.zsend, self.zrecv, self.ysend, self.yrecv = zsend, zrecv, ysend, yrecv
        self.me, self.z, self.y = place()

    def mine(self, way, step, chunk):
        sign = 1 if way == 0 else -1
        dest = lax.rem(self.z + sign * (4 - step) + 2 * NZ, NZ)
        return pl.ds(pl.multiple_of(dest * LINE + chunk * HALF, HALF), HALF)

    def hop(self, way, step, chunk):
        sign = 1 if way == 0 else -1
        part = pl.ds(chunk * HALF, HALF)
        first = 0 if chunk == way else 1
        if step == first:
            source = self.src.at[self.mine(way, step, chunk)]
        else:
            source = self.slots.at[way, step - 1, part]
        return remote(
            source,
            self.slots.at[way, step, part],
            self.zsend.at[way, step, chunk],
            self.zrecv.at[way, step, chunk],
            to_expert(self.z + sign, self.y),
        )

    def step(self, s):
        for chunk in (0, 1):
            for way in (0, 1):
                first = 0 if chunk == way else 1
                part = pl.ds(chunk * HALF, HALF)
                if s < first:
                    continue
                if s > first:
                    self.hop(way, s - 1, chunk).wait_recv()
                    if s < 4:
                        self.slots[way, s - 1, part] = (
                            self.slots[way, s - 1, part].astype(F32)
                            + self.src[self.mine(way, s, chunk)].astype(F32)
                        ).astype(BF16)
                if s < 4:
                    self.hop(way, s, chunk).start()

    def line(self, d):
        target = lax.rem(self.y + d, NY)
        return remote(
            self.line_buf.at[pl.ds(pl.multiple_of(target * TOK, TOK), TOK)],
            self.line_slots.at[d - 1],
            self.ysend.at[d - 1],
            self.yrecv.at[d - 1],
            to_expert(self.z, self.y + d),
        )

    def cross(self):
        for chunk in (0, 1):
            part = pl.ds(chunk * HALF, HALF)
            own = self.src[pl.ds(pl.multiple_of(self.z * LINE + chunk * HALF, HALF), HALF)]
            self.line_buf[part] = (
                own.astype(F32)
                + self.slots[0, 3, part].astype(F32)
                + self.slots[1, 3, part].astype(F32)
            ).astype(BF16)
        for d in (1, 2, 3):
            self.line(d).start()

    def total(self):
        for d in (1, 2, 3):
            self.line(d).wait_recv()
        result = self.line_buf[pl.ds(pl.multiple_of(self.y * TOK, TOK), TOK)].astype(F32)
        for d in (1, 2, 3):
            result = result + self.line_slots[d - 1].astype(F32)
        return result

    def finish(self):
        for chunk in (0, 1):
            for way in (0, 1):
                for s in range(0 if chunk == way else 1, 4):
                    self.hop(way, s, chunk).wait_send()
        for d in (1, 2, 3):
            self.line(d).wait_send()


SCATTER_SCRATCH = [
    pltpu.VMEM((2, 4, LINE, D), BF16),
    pltpu.VMEM((LINE, D), BF16),
    pltpu.VMEM((3, TOK, D), BF16),
    pltpu.SemaphoreType.DMA((2, 4, 2)),
    pltpu.SemaphoreType.DMA((2, 4, 2)),
    pltpu.SemaphoreType.DMA((3,)),
    pltpu.SemaphoreType.DMA((3,)),
]

PIECE_ROWS = 32
PIECE_COLS = 128


def piece(ref, index):
    row = pl.multiple_of(lax.div(index, 8) * PIECE_ROWS, PIECE_ROWS)
    col = pl.multiple_of(lax.rem(index, 8) * PIECE_COLS, PIECE_COLS)
    return ref.at[pl.ds(row, PIECE_ROWS), pl.ds(col, PIECE_COLS)]


class Sections:
    def __init__(self, memory, term_rows, terms, total, bsend, brecv, tsend, trecv, gsend, grecv, psend, precv):
        self.memory, self.term_rows, self.terms, self.sum_rows = memory, term_rows, terms, total
        self.bsend, self.brecv, self.tsend, self.trecv = bsend, brecv, tsend, trecv
        self.gsend, self.grecv, self.psend, self.precv = gsend, grecv, psend, precv
        self.s = lax.axis_index("section")
        self.is_root = self.s == ROOT
        self.is_leader = lax.rem(self.s, 4) == ROOT % 4

    def spread(self, slot, d):
        return remote(self.memory, self.memory, self.bsend.at[slot], self.brecv, to_section(self.s + d))

    def spread_root(self, middle):
        @pl.when(self.is_root)
        def _():
            self.memory[...] = middle[...]
            for slot in (0, 1, 2):
                self.spread(slot, 4 * (slot + 1)).start()

    def spread_leader(self):
        @pl.when(self.is_leader & jnp.logical_not(self.is_root))
        def _():
            self.spread(0, 4).wait_recv()

        @pl.when(self.is_leader)
        def _():
            for slot, d in ((3, -2), (4, -1), (5, 1)):
                self.spread(slot, d).start()

    def spread_wait(self):
        @pl.when(jnp.logical_not(self.is_leader))
        def _():
            self.spread(0, 4).wait_recv()

    def spread_finish(self):
        @pl.when(self.is_root)
        def _():
            for slot in (0, 1, 2):
                self.spread(slot, 4).wait_send()

        @pl.when(self.is_leader)
        def _():
            for slot in (3, 4, 5):
                self.spread(slot, 1).wait_send()

    def term(self, d):
        target = lax.rem(self.s + d, NSEC)
        return remote(
            piece(self.term_rows, target),
            self.terms.at[d - 1],
            self.tsend.at[d - 1],
            self.trecv.at[d - 1],
            to_section(self.s + d),
        )

    def terms_begin(self):
        for d in range(1, NSEC):
            self.term(d).start()

    def result(self, d, arriving):
        index = lax.rem(self.s + NSEC - d, NSEC) if arriving else self.s
        view = piece(self.sum_rows, index)
        return remote(view, view, self.gsend.at[d - 1], self.grecv.at[d - 1], to_section(self.s + d))

    def terms_sum(self):
        own = piece(self.term_rows, self.s)[...].astype(F32)
        for d in range(1, NSEC):
            self.term(d).wait_recv()
            own = own + self.terms[d - 1].astype(F32)
        view = piece(self.sum_rows, self.s)
        view[...] = own.astype(BF16)
        for d in range(1, NSEC):
            self.result(d, False).start()

    def terms_finish(self):
        for d in range(1, NSEC):
            self.result(d, True).wait_recv()
        for d in range(1, NSEC):
            self.term(d).wait_send()
            self.result(d, False).wait_send()

    def passing(self, src, dst, d, slot):
        return remote(src, dst, self.psend.at[slot], self.precv.at[slot], to_section(self.s + d))


def kernel(
    hidden_a, hidden_b, mid_b, cotangent, mem_saved, lengths,
    routes_f, routes_b, probs_f, probs_b, gains, w_in, w_out, w_query, w_keyval, w_output,
    rows_out, grads_out, memory_grad_out,
    all_query, all_keyval, all_output, all_shares, all_a, all_x, all_d, part_a, part_b,
    query, key, value, mixed, middle, upstream, out_rows, grad_rows,
    memory, term_rows, terms, *sems
):
    sems = list(sems)

    def take(count):
        taken = sems[:count]
        del sems[:count]
        return taken

    me, z, y = place()
    my_expert = lax.div(me, NZ)
    section = lax.axis_index("section")
    is_decoder = section >= FIRST_DECODER
    gain_moe = gains[0:1, :]
    gain_att = gains[1:2, :]

    g_wo = Gather(all_output, 16, 0, D, *take(4))
    g_wq = Gather(all_query, 32, 0, INNER, *take(4))
    g_wkv = Gather(all_keyval, 32, 0, D, *take(4))
    g_sh = Gather(all_shares, 8, 0, 128, *take(4))
    g_a = [Gather(all_a, TOK, c * 512, 512, *take(4)) for c in (0, 1)]
    g_x = [Gather(all_x, TOK, c * 512, 512, *take(4)) for c in (0, 1)]
    g_d = [Gather(all_d, TOK, c * 512, 512, *take(4)) for c in (0, 1)]
    scatter_a = Scatter(part_a, *take(7))
    scatter_b = Scatter(part_b, *take(7))
    sections = Sections(memory, term_rows, terms, memory_grad_out, *take(8))

    partners = (
        [to_expert(z + 1, y), to_expert(z - 1, y)]
        + [to_expert(z, y + d) for d in (1, 2, 3)]
        + [to_section(section + d) for d in range(1, NSEC)]
    )
    barrier = pltpu.get_barrier_semaphore()
    for device in partners:
        pl.semaphore_signal(barrier, inc=1, device_id=device, device_id_type=MESH)

    def own_rows(ref, size):
        return ref.at[pl.ds(pl.multiple_of(me * size, size), size)]

    own_rows(all_output, 16)[...] = w_output[...]
    own_rows(all_query, 32)[...] = w_query[...]
    own_rows(all_keyval, 32)[...] = w_keyval[...]
    own_rows(all_a, TOK)[...] = norm_rows(hidden_a[...], gain_moe)
    own_rows(all_x, TOK)[...] = norm_rows(hidden_b[...], gain_moe)
    own_shares = own_rows(all_shares, 8)
    own_shares[...] = jnp.zeros((8, 128), F32)
    for base, routes, probs, line in ((0, routes_f, probs_f, 0), (4, routes_b, probs_b, 2)):
        live = live_column(
            jnp.where(is_decoder, lengths[line + 1, 0], lengths[line, 0]),
            jnp.where(is_decoder, lengths[line + 1, 1], lengths[line, 1]),
        )
        for e in range(EXPERTS):
            share = jnp.where(routes[:, 0:1] == e, probs[:, 0:1], 0.0) + jnp.where(
                routes[:, 1:2] == e, probs[:, 1:2], 0.0
            )
            own_shares[base + e : base + e + 1, 0:TOK] = turned(share * live)
    pl.semaphore_wait(barrier, len(partners))

    def share_column(block, i, base):
        row = all_shares[pl.ds((block * NY + i) * 8 + base + my_expert, 1), 0:TOK]
        return upright(row)

    def line_rows(block):
        return pl.ds(pl.multiple_of(block * LINE, LINE), LINE)

    def expert_forward(block, _):
        units = gelu_value(dot_nn(all_a[line_rows(block)], w_in[...])).astype(BF16)
        part = dot_nn(units, w_out[...])
        for i in range(NY):
            part_a[pl.ds(pl.multiple_of(block * LINE + i * TOK, TOK), TOK)] = (
                part[i * TOK : (i + 1) * TOK] * share_column(block, i, 0)
            ).astype(BF16)
        return 0

    def expert_backward(block, _):
        for i in range(NY):
            part = pl.ds(pl.multiple_of(block * LINE + i * TOK, TOK), TOK)
            all_d_row = all_d[part].astype(F32) * share_column(block, i, 4)
            part_b[part] = all_d_row.astype(BF16)
        through = dot_nt(part_b[line_rows(block)], w_out[...])
        slope = gelu_slope(dot_nn(all_x[line_rows(block)], w_in[...]))
        unit_grad = (through * slope).astype(BF16)
        part_b[line_rows(block)] = dot_nt(unit_grad, w_in[...]).astype(BF16)
        return 0

    def project(mid_rows, mem_rows):
        query[...] = dot_nn(norm_rows(mid_rows, gain_att), all_query[...]).astype(BF16)
        key[...] = dot_nn(mem_rows, all_keyval[:, :INNER]).astype(BF16)
        value[...] = dot_nn(mem_rows, all_keyval[:, INNER:]).astype(BF16)

    def mix_grads(pairs):
        allowed = allowed_keys(lengths[2, 0], lengths[2, 1])
        for p in pairs:
            at = slice(p * PAIR, (p + 1) * PAIR)
            grads = mix_pair_grad(query[:, at], key[:, at], value[:, at], mixed[:, at], allowed)
            query[:, at], key[:, at], value[:, at] = grads

    def attend_grads():
        d_normed = dot_nt(query[...], all_query[...]).astype(BF16).astype(F32)
        d_memory = dot_nt(key[...], all_keyval[:, :INNER]) + dot_nt(value[...], all_keyval[:, INNER:])
        term_rows[...] = jnp.where(is_decoder, d_memory, 0.0).astype(BF16)
        through = norm_grad(mid_b[...], gain_att, d_normed).astype(BF16).astype(F32)
        cot = cotangent[...].astype(F32)
        upstream[...] = jnp.where(is_decoder, cot + through, cot).astype(BF16)
        own_rows(all_d, TOK)[...] = upstream[...]

    weights, side_a = [g_wo, g_wq, g_wkv], [g_sh] + g_a
    for g in weights + side_a + g_x:
        g.begin()
    for s in range(4):
        for g in weights:
            g.step(s)
    for g in side_a:
        g.step(0)
    for g in weights:
        g.step(4)

    for s in range(1, 4):
        for g in side_a:
            g.step(s)
        if s == 1:
            project(mid_b[...], mem_saved[...])
            mixed[...] = dot_nt(cotangent[...], all_output[...]).astype(BF16)
        else:
            mix_grads((0, 1) if s == 2 else (2, 3))
    for g in g_x:
        g.step(0)
    attend_grads()
    for g in g_d:
        g.begin()
    sections.terms_begin()
    for g in side_a:
        g.step(4)

    for s in range(1, 4):
        for g in g_x:
            g.step(s)
        lax.fori_loop(2 * s - 2, 2 * s, expert_forward, 0)
    for g in g_d:
        g.step(0)
    for g in g_x:
        g.step(4)
    lax.fori_loop(6, 8, expert_forward, 0)

    g_d[0].step(1)
    g_d[1].step(1)
    sections.terms_sum()
    for s in range(2, 4):
        for g in g_d:
            g.step(s)
    scatter_a.step(0)
    for g in g_d:
        g.step(4)

    lax.fori_loop(0, 2, expert_backward, 0)
    scatter_a.step(1)
    lax.fori_loop(2, 4, expert_backward, 0)
    scatter_a.step(2)
    lax.fori_loop(4, 6, expert_backward, 0)
    scatter_a.step(3)
    lax.fori_loop(6, 8, expert_backward, 0)
    scatter_b.step(0)
    scatter_a.step(4)
    scatter_a.cross()

    scatter_b.step(1)
    middle[...] = (hidden_a[...].astype(F32) + scatter_a.total()).astype(BF16)
    sections.spread_root(middle)
    sections.spread_leader()
    scatter_b.step(2)
    sections.spread_wait()
    project(middle[...], memory[...])
    allowed = allowed_keys(lengths[0, 0], lengths[0, 1])
    for p in range(INNER // PAIR):
        at = slice(p * PAIR, (p + 1) * PAIR)
        mixed[:, at] = mix_pair(query[:, at], key[:, at], value[:, at], allowed)
    scatter_b.step(3)
    projected = jnp.where(is_decoder, dot_nn(mixed[...], all_output[...]), 0.0)
    out_rows[...] = (middle[...].astype(F32) + projected).astype(BF16)
    ahead = sections.passing(out_rows, rows_out, 1, 0)
    ahead.start()
    scatter_b.step(4)
    scatter_b.cross()
    sections.terms_finish()
    for g in weights + side_a + g_x + g_d:
        g.finish()
    scatter_a.finish()
    sections.spread_finish()
    through = norm_grad(hidden_b[...], gain_moe, scatter_b.total())
    grad_rows[...] = (upstream[...].astype(F32) + through).astype(BF16)
    behind = sections.passing(grad_rows, grads_out, -1, 1)
    behind.start()
    scatter_b.finish()
    ahead.wait()
    behind.wait()


def on_device(
    hidden_fwd,
    hidden_bwd,
    mid_bwd,
    grads_in,
    memory_saved,
    lengths,
    routes_fwd,
    routes_bwd,
    probs_fwd,
    probs_bwd,
    norm_gains,
    w_in,
    w_out,
    w_query,
    w_keyval,
    w_output,
):
    shape = jax.ShapeDtypeStruct((TOK, D), BF16)
    vmem = pl.BlockSpec(memory_space=pltpu.VMEM)
    smem = pl.BlockSpec(memory_space=pltpu.SMEM)
    row_buf = pltpu.VMEM((ROWS, D), BF16)
    tok_buf = pltpu.VMEM((TOK, D), BF16)
    inner_buf = pltpu.VMEM((TOK, INNER), BF16)
    passed_rows, passed_grads, memory_grad = pl.pallas_call(
        kernel,
        out_shape=[shape] * 3,
        in_specs=[vmem] * 5 + [smem] + [vmem] * 10,
        out_specs=[vmem] * 3,
        scratch_shapes=[
            pltpu.VMEM((D, INNER), BF16),
            pltpu.VMEM((D, 2 * INNER), BF16),
            pltpu.VMEM((INNER, D), BF16),
            pltpu.VMEM((NZ * NY * 8, 128), F32),
            row_buf,
            row_buf,
            row_buf,
            row_buf,
            row_buf,
            inner_buf,
            inner_buf,
            inner_buf,
            inner_buf,
            tok_buf,
            tok_buf,
            tok_buf,
            tok_buf,
            tok_buf,
            tok_buf,
            pltpu.VMEM((NSEC - 1, PIECE_ROWS, PIECE_COLS), BF16),
        ]
        + GATHER_SEMS * 10
        + SCATTER_SCRATCH * 2
        + [
            pltpu.SemaphoreType.DMA((6,)),
            pltpu.SemaphoreType.DMA,
            pltpu.SemaphoreType.DMA((NSEC - 1,)),
            pltpu.SemaphoreType.DMA((NSEC - 1,)),
            pltpu.SemaphoreType.DMA((NSEC - 1,)),
            pltpu.SemaphoreType.DMA((NSEC - 1,)),
            pltpu.SemaphoreType.DMA((2,)),
            pltpu.SemaphoreType.DMA((2,)),
        ],
        compiler_params=pltpu.CompilerParams(
            collective_id=0, has_side_effects=True, vmem_limit_bytes=56 * 2**20
        ),
        name="relay_step",
    )(
        hidden_fwd[0],
        hidden_bwd[0],
        mid_bwd[0],
        grads_in[0],
        memory_saved,
        lengths,
        routes_fwd[0],
        routes_bwd[0],
        probs_fwd[0],
        probs_bwd[0],
        norm_gains[0],
        w_in[0],
        w_out[0],
        w_query[0],
        w_keyval[0],
        w_output[0],
    )
    return (passed_rows[None], passed_grads[None], memory_grad)


def solution(mesh):
    return jax.shard_map(
        on_device,
        mesh=mesh,
        in_specs=(
            P("section", "expert", None),
            P("section", "expert", None),
            P("section", "expert", None),
            P("section", "expert", None),
            P("expert", None),
            P(None, "expert"),
            P("section", "expert", None),
            P("section", "expert", None),
            P("section", "expert", None),
            P("section", "expert", None),
            P("section", None, None),
            P("section", None, "expert"),
            P("section", "expert", None),
            P("section", "expert", None),
            P("section", "expert", None),
            P("section", "expert", None),
        ),
        out_specs=(P("section", "expert", None), P("section", "expert", None), P("expert", None)),
        check_vma=False,
    )
```

time: 894 us -> 301 us (0.34)
  the two profiles are of different devices: /device:TPU:55 before, /device:TPU:59 now
where the time goes in v2:
time: 301 us
  Pallas kernels  293 us (97%)
  local copies, waits for them, and re-layouts  7.4 us (2%)
    pallas_call x1, Pallas kernels, on_device(): pl.pallas_call(kernel, out_shape=[shape] * 3, in_specs=[vmem] * 5 + [smem...  293 us

profile of v2, /device:TPU:59, one launch (start us, length us, event | category | flops | bytes accessed | tf_op | source)
XLA Modules:
  0.0 300.8 jit_solution(9135983603732883244)
XLA Ops:
  0.6 0.0 copy-start.2
  0.6 0.7 copy-done.2
  1.3 0.0 copy-start.3
  1.3 0.7 copy.19.lengths
  2.0 0.0 copy-done.3
  2.0 0.0 copy-start.4
  2.0 0.7 copy.20.routes_f
  2.7 0.0 copy-done.4
  2.7 0.0 copy-start.5
  2.7 0.7 copy.21.routes_b
  3.4 0.0 copy-done.5
  3.4 0.0 copy-start.6
  3.4 0.7 copy.22.probs_f
  4.1 0.0 copy-done.6
  4.1 0.7 copy.23.probs_b
  4.8 292.8 %relay_step.1 = (bf16[64,1024]{1,0:T(8,128)(2,1)}, bf16[64,1024]{1,0:T(8,128)(2,1)}, bf16[64,1024]{1,0:T(8,128)(2,1)}) custom-call(bf16[64,1024]{1,0:T(8,128)(2,1)} %bitcast.18, bf16[64,1024]{1,0:T(8,128)(2,1)} %bitcast.19, bf16[64,1024]{1,0:T(8,128)(2,1)} %bitcast.20, bf16[64,1024]{1,0:T(8,128)(2,1)} %bitcast.21, bf16[64,1024]{1,0:T(8,128)(2,1)} %mem_saved.1, ...), custom_call_target="tpu_custom_call" | custom-call | tf_op jit(solution)/shard_map/relay_step/pallas_call | solution.py:638
  297.6 0.0 copy-start.1
  297.6 1.6 copy.27
  299.2 0.0 copy-done.1
  299.2 0.0 copy-start
  299.2 0.7 copy.28
  299.9 0.3 copy-done
  300.2 0.7 copy.29
Async XLA Ops:
  0.6 0.7 copy-start.2
  1.3 0.7 copy-start.3
  2.0 0.7 copy-start.4
  2.7 0.7 copy-start.5
  3.4 0.7 copy-start.6
  297.6 1.6 copy-start.1
  299.2 1.0 copy-start

commit v3 on v2

v3 whole, which is shorter than its diff:
```python
import functools

import jax
import jax.numpy as jnp
from jax import lax
from jax.experimental import pallas as pl
from jax.experimental.pallas import tpu as pltpu
from jax.sharding import PartitionSpec as P

MESH = pl.DeviceIdType.MESH
BF16 = jnp.bfloat16
F32 = jnp.float32
HEAD_DIM = 64
EXPERTS = 4
SEQ = 32
NZ = 8
NY = 4
NSEC = 16
FIRST_DECODER = 3
ROOT = FIRST_DECODER - 1
TOK = 64
LINE = NY * TOK
D = 1024
CUT_A, CUT_X, CUT_D, CUT_RA, CUT_RB = 768, 896, 768, 768, 896
UNITS = 512
INNER = 512
PAIR = 2 * HEAD_DIM

EPS = 1e-05
ROOT_HALF = 0.7071067811865476
INV_ROOT_TWO_PI = 0.3989422804014327


def dot_nn(a, b):
    return lax.dot_general(a, b, (((1,), (0,)), ((), ())), preferred_element_type=F32)


def dot_nt(a, b):
    return lax.dot_general(a, b, (((1,), (1,)), ((), ())), preferred_element_type=F32)


def dot_tn(a, b):
    return lax.dot_general(a, b, (((0,), (0,)), ((), ())), preferred_element_type=F32)


def norm_parts(row_block):
    values = row_block.astype(F32)
    center = values - jnp.mean(values, axis=-1, keepdims=True)
    spread = jnp.mean(center * center, axis=-1, keepdims=True)
    scale = lax.rsqrt(spread + EPS)
    return center * scale, scale


def norm_rows(row_block, gain_row):
    return (norm_parts(row_block)[0] * gain_row).astype(BF16)


def norm_grad(row_block, gain_row, upstream):
    unit, scale = norm_parts(row_block)
    grad = upstream * gain_row
    mean_grad = jnp.mean(grad, axis=-1, keepdims=True)
    mean_along = jnp.mean(grad * unit, axis=-1, keepdims=True)
    return scale * (grad - mean_grad - unit * mean_along)


def gelu_value(inputs):
    return 0.5 * inputs * (1.0 + lax.erf(inputs * ROOT_HALF))


def gelu_slope(inputs):
    return (
        0.5 * (1.0 + lax.erf(inputs * ROOT_HALF))
        + inputs * jnp.exp(-0.5 * inputs * inputs) * INV_ROOT_TWO_PI
    )


def allowed_keys(len_first, len_second):
    row = lax.broadcasted_iota(jnp.int32, (TOK, TOK), 0)
    col = lax.broadcasted_iota(jnp.int32, (TOK, TOK), 1)
    col_len = jnp.where(col < SEQ, len_first, len_second)
    same = (row < SEQ) == (col < SEQ)
    return same & (jnp.where(col < SEQ, col, col - SEQ) < col_len)


def live_row(len_first, len_second):
    col = lax.broadcasted_iota(jnp.int32, (1, TOK), 1)
    col_len = jnp.where(col < SEQ, len_first, len_second)
    return jnp.where(jnp.where(col < SEQ, col, col - SEQ) < col_len, 1.0, 0.0)


def one_head(values, side):
    lane = lax.broadcasted_iota(jnp.int32, values.shape, 1)
    return jnp.where((lane < HEAD_DIM) == (side == 0), values, jnp.zeros_like(values))


def head_weights(query, key, allowed):
    scores = dot_nt(query, key) * HEAD_DIM ** (-0.5)
    raised = jnp.where(allowed, jnp.exp(scores), 0.0)
    return raised / jnp.sum(raised, axis=-1, keepdims=True)


def mix_pair(query, key, value, allowed):
    mixed = jnp.zeros((TOK, PAIR), F32)
    for side in (0, 1):
        weights = head_weights(one_head(query, side), key, allowed).astype(BF16)
        mixed = mixed + dot_nn(weights, one_head(value, side))
    return mixed.astype(BF16)


def mix_pair_grad(query, key, value, d_mixed, allowed):
    d_query = jnp.zeros((TOK, PAIR), F32)
    d_key = jnp.zeros((TOK, PAIR), F32)
    d_value = jnp.zeros((TOK, PAIR), F32)
    for side in (0, 1):
        query_one, grad_one = one_head(query, side), one_head(d_mixed, side)
        exact = head_weights(query_one, key, allowed)
        d_weights = dot_nt(grad_one, value).astype(BF16).astype(F32)
        d_value = d_value + dot_tn(exact.astype(BF16), grad_one)
        along = jnp.sum(d_weights * exact, axis=-1, keepdims=True)
        d_scores = (exact * (d_weights - along) * HEAD_DIM ** (-0.5)).astype(BF16)
        d_query = d_query + dot_nn(d_scores, one_head(key, side))
        d_key = d_key + dot_tn(d_scores, query_one)
    return d_query.astype(BF16), d_key.astype(BF16), d_value.astype(BF16)


def upright(row):
    eye = lax.broadcasted_iota(jnp.int32, (TOK, TOK), 0) == lax.broadcasted_iota(
        jnp.int32, (TOK, TOK), 1
    )
    return jnp.sum(jnp.where(eye, row, 0.0), axis=1, keepdims=True)


def place():
    me = lax.axis_index("expert")
    return me, lax.div(me, NY), lax.rem(me, NY)


def to_expert(z, y):
    return {"expert": lax.rem(z + 2 * NZ, NZ) * NY + lax.rem(y + 2 * NY, NY)}


def to_section(s):
    return {"section": lax.rem(s + 2 * NSEC, NSEC)}


def remote(src, dst, send, recv, device):
    return pltpu.make_async_remote_copy(
        src_ref=src, dst_ref=dst, send_sem=send, recv_sem=recv, device_id=device, device_id_type=MESH
    )


class Ring:
    def __init__(self, view, send, recv):
        self.view, self.send, self.recv = view, send, recv
        _, self.z, self.y = place()

    def hop(self, way, step, arriving):
        sign = 1 if way == 0 else -1
        back = step + 1 if arriving else step
        origin = lax.rem(self.z - sign * back + 2 * NZ, NZ)
        block = self.view(origin, way if step == 3 else None)
        return remote(
            block, block, self.send.at[way, step], self.recv.at[way, step], to_expert(self.z + sign, self.y)
        )

    def step(self, s):
        for way in (0, 1):
            if s > 0:
                self.hop(way, s - 1, True).wait_recv()
            if s < 4:
                self.hop(way, s, False).start()

    def finish(self):
        for way in (0, 1):
            for s in range(4):
                self.hop(way, s, False).wait_send()


class Line:
    def __init__(self, view, send, recv):
        self.view, self.send, self.recv = view, send, recv
        _, self.z, self.y = place()

    def copy(self, d, arriving):
        block = self.view(lax.rem(self.y + NY - d, NY) if arriving else self.y)
        return remote(block, block, self.send.at[d - 1], self.recv.at[d - 1], to_expert(self.z, self.y + d))

    def begin(self):
        for d in (1, 2, 3):
            self.copy(d, False).start()

    def arrive(self):
        for d in (1, 2, 3):
            self.copy(d, True).wait_recv()

    def finish(self):
        for d in (1, 2, 3):
            self.copy(d, False).wait_send()


def halves(cut):
    first = (cut // 128 + 1) // 2 * 128
    return (0, first), (first, cut - first)


class Gather:
    def __init__(self, array, first_col, cols, ysend, yrecv, zsend, zrecv):
        _, z, _ = place()
        at = pl.ds(first_col, cols)
        self.line = Line(lambda y: array.at[z, y, :, at], ysend, yrecv)

        def view(origin, half):
            if half is None:
                return array.at[origin, :, :, at]
            return array.at[origin, pl.ds(half * 2, 2), :, at]

        self.ring = Ring(view, zsend, zrecv)

    def begin(self):
        self.line.begin()

    def step(self, s):
        if s == 0:
            self.line.arrive()
        self.ring.step(s)

    def finish(self):
        self.line.finish()
        self.ring.finish()


class CrossGather:
    def __init__(self, array, first_col, cols, ysend, yrecv, zsend, zrecv):
        _, _, me_y = place()
        at = pl.ds(first_col, cols)
        rows = array.shape[2] // 2

        def view(origin, half):
            if half is None:
                return array.at[origin, me_y, :, at]
            return array.at[origin, me_y, pl.ds(half * rows, rows), at]

        self.ring = Ring(view, zsend, zrecv)
        self.line = Line(lambda y: array.at[:, y, :, at], ysend, yrecv)

    def step(self, s):
        self.ring.step(s)

    def begin_line(self):
        self.line.begin()

    def arrive(self):
        self.line.arrive()

    def finish(self):
        self.ring.finish()
        self.line.finish()


GATHER_SEMS = [
    pltpu.SemaphoreType.DMA((3,)),
    pltpu.SemaphoreType.DMA((3,)),
    pltpu.SemaphoreType.DMA((2, 4)),
    pltpu.SemaphoreType.DMA((2, 4)),
]


class SumRing:
    def __init__(self, own, slot, send, recv):
        self.own, self.slot, self.send, self.recv = own, slot, send, recv
        _, self.z, self.y = place()

    def term(self, way, step, chunk):
        sign = 1 if way == 0 else -1
        return self.own(lax.rem(self.z + sign * (4 - step) + 2 * NZ, NZ), chunk)

    def hop(self, way, step, chunk):
        first = 0 if chunk == way else 1
        source = self.term(way, step, chunk) if step == first else self.slot(way, step - 1, chunk)
        return remote(
            source,
            self.slot(way, step, chunk),
            self.send.at[way, step, chunk],
            self.recv.at[way, step, chunk],
            to_expert(self.z + (1 if way == 0 else -1), self.y),
        )

    def step(self, s, chunks=(0, 1)):
        for chunk in chunks:
            for way in (0, 1):
                first = 0 if chunk == way else 1
                if s < first:
                    continue
                if s > first:
                    self.hop(way, s - 1, chunk).wait_recv()
                    if s < 4:
                        slot = self.slot(way, s - 1, chunk)
                        slot[...] = (
                            slot[...].astype(F32) + self.term(way, s, chunk)[...].astype(F32)
                        ).astype(BF16)
                if s < 4:
                    self.hop(way, s, chunk).start()

    def total(self, chunk):
        return (
            self.own(self.z, chunk)[...].astype(F32)
            + self.slot(0, 3, chunk)[...].astype(F32)
            + self.slot(1, 3, chunk)[...].astype(F32)
        )

    def finish(self):
        for chunk in (0, 1):
            for way in (0, 1):
                for s in range(0 if chunk == way else 1, 4):
                    self.hop(way, s, chunk).wait_send()


class SumLine:
    def __init__(self, src, slot, send, recv):
        self.src, self.slot, self.send, self.recv = src, slot, send, recv
        _, self.z, self.y = place()

    def copy(self, d, chunk):
        return remote(
            self.src(lax.rem(self.y + d, NY), chunk),
            self.slot(d, chunk),
            self.send.at[chunk, d - 1],
            self.recv.at[chunk, d - 1],
            to_expert(self.z, self.y + d),
        )

    def begin(self, chunk):
        for d in (1, 2, 3):
            self.copy(d, chunk).start()

    def arrive(self):
        for chunk in (0, 1):
            for d in (1, 2, 3):
                self.copy(d, chunk).wait_recv()

    def finish(self):
        for chunk in (0, 1):
            for d in (1, 2, 3):
                self.copy(d, chunk).wait_send()


class DirectSum:
    def __init__(self, src, slots, send, recv):
        self.src, self.slots, self.send, self.recv = src, slots, send, recv
        _, self.z, self.y = place()

    def copy(self, d):
        return remote(
            self.src(lax.rem(self.y + d, NY)),
            self.slots.at[d - 1],
            self.send.at[d - 1],
            self.recv.at[d - 1],
            to_expert(self.z, self.y + d),
        )

    def begin(self):
        for d in (1, 2, 3):
            self.copy(d).start()

    def total(self, sums):
        for d in (1, 2, 3):
            self.copy(d).wait_recv()
        own = self.src(self.y)

        def add(block, _):
            result = own[block].astype(F32)
            for d in (1, 2, 3):
                result = result + self.slots[d - 1, block].astype(F32)
            sums[block] = result.astype(BF16)
            return 0

        lax.fori_loop(0, NZ, add, 0)

    def finish(self):
        for d in (1, 2, 3):
            self.copy(d).wait_send()


class Scatter:
    def __init__(self, cut, src, slots, line_buf, line_slots, zsend, zrecv, ysend, yrecv):
        def part(chunk):
            return pl.ds(*halves(cut)[chunk])

        self.part, self.line_buf, self.line_slots = part, line_buf, line_slots
        self.ring = SumRing(
            lambda dest, chunk: src.at[dest, :, :, part(chunk)],
            lambda way, step, chunk: slots.at[way, step, :, :, part(chunk)],
            zsend,
            zrecv,
        )
        self.line = SumLine(
            lambda y, chunk: line_buf.at[y, :, part(chunk)],
            lambda d, chunk: line_slots.at[d - 1, :, part(chunk)],
            ysend,
            yrecv,
        )

    def step(self, s):
        self.ring.step(s)

    def cross(self):
        for chunk in (0, 1):
            self.ring.step(4, (chunk,))
            self.line_buf[:, :, self.part(chunk)] = self.ring.total(chunk).astype(BF16)
            self.line.begin(chunk)

    def total(self):
        self.line.arrive()
        result = self.line_buf[self.line.y].astype(F32)
        for d in (1, 2, 3):
            result = result + self.line_slots[d - 1].astype(F32)
        return result

    def finish(self):
        self.ring.finish()
        self.line.finish()


class CrossScatter:
    def __init__(self, cut, src, line_slots, sums, slots, ysend, yrecv, zsend, zrecv):
        at = pl.ds(cut, D - cut)
        self.sums = sums
        self.line = DirectSum(lambda y: src.at[:, y, :, at], line_slots, ysend, yrecv)
        self.ring = SumRing(
            lambda dest, chunk: sums.at[dest, pl.ds(chunk * 32, 32)],
            lambda way, step, chunk: slots.at[way, step, pl.ds(chunk * 32, 32)],
            zsend,
            zrecv,
        )

    def begin(self):
        self.line.begin()

    def sum_line(self):
        self.line.total(self.sums)

    def step(self, s):
        self.ring.step(s)

    def total(self):
        return jnp.concatenate([self.ring.total(0), self.ring.total(1)], axis=0)

    def finish(self):
        self.line.finish()
        self.ring.finish()


def scatter_scratch(cut):
    return [
        pltpu.VMEM((2, 4, NY, TOK, cut), BF16),
        pltpu.VMEM((NY, TOK, cut), BF16),
        pltpu.VMEM((3, TOK, cut), BF16),
    ] + [pltpu.SemaphoreType.DMA(dims) for dims in ((2, 4, 2), (2, 4, 2), (2, 3), (2, 3))]


def cross_scratch(cut):
    return [
        pltpu.VMEM((3, NZ, TOK, D - cut), BF16),
        pltpu.VMEM((NZ, TOK, D - cut), BF16),
        pltpu.VMEM((2, 4, TOK, D - cut), BF16),
    ] + [pltpu.SemaphoreType.DMA(dims) for dims in ((3,), (3,), (2, 4, 2), (2, 4, 2))]


PIECE_ROWS = 32
PIECE_COLS = 128


def piece(ref, index):
    row = pl.multiple_of(lax.div(index, 8) * PIECE_ROWS, PIECE_ROWS)
    col = pl.multiple_of(lax.rem(index, 8) * PIECE_COLS, PIECE_COLS)
    return ref.at[pl.ds(row, PIECE_ROWS), pl.ds(col, PIECE_COLS)]


class Sections:
    def __init__(self, memory, term_rows, terms, total, bsend, brecv, tsend, trecv, gsend, grecv, psend, precv):
        self.memory, self.term_rows, self.terms, self.sum_rows = memory, term_rows, terms, total
        self.bsend, self.brecv, self.tsend, self.trecv = bsend, brecv, tsend, trecv
        self.gsend, self.grecv, self.psend, self.precv = gsend, grecv, psend, precv
        self.s = lax.axis_index("section")
        self.is_root = self.s == ROOT
        self.is_leader = lax.rem(self.s, 4) == ROOT % 4

    def spread(self, slot, d):
        return remote(self.memory, self.memory, self.bsend.at[slot], self.brecv, to_section(self.s + d))

    def spread_root(self, middle):
        @pl.when(self.is_root)
        def _():
            self.memory[...] = middle[...]
            for slot in (0, 1, 2):
                self.spread(slot, 4 * (slot + 1)).start()

    def spread_leader(self):
        @pl.when(self.is_leader & jnp.logical_not(self.is_root))
        def _():
            self.spread(0, 4).wait_recv()

        @pl.when(self.is_leader)
        def _():
            for slot, d in ((3, -2), (4, -1), (5, 1)):
                self.spread(slot, d).start()

    def spread_wait(self):
        @pl.when(jnp.logical_not(self.is_leader))
        def _():
            self.spread(0, 4).wait_recv()

    def spread_finish(self):
        @pl.when(self.is_root)
        def _():
            for slot in (0, 1, 2):
                self.spread(slot, 4).wait_send()

        @pl.when(self.is_leader)
        def _():
            for slot in (3, 4, 5):
                self.spread(slot, 1).wait_send()

    def term(self, d):
        target = lax.rem(self.s + d, NSEC)
        return remote(
            piece(self.term_rows, target),
            self.terms.at[d - 1],
            self.tsend.at[d - 1],
            self.trecv.at[d - 1],
            to_section(self.s + d),
        )

    def terms_begin(self):
        for d in range(1, NSEC):
            self.term(d).start()

    def result(self, d, arriving):
        index = lax.rem(self.s + NSEC - d, NSEC) if arriving else self.s
        view = piece(self.sum_rows, index)
        return remote(view, view, self.gsend.at[d - 1], self.grecv.at[d - 1], to_section(self.s + d))

    def terms_sum(self):
        own = piece(self.term_rows, self.s)[...].astype(F32)
        for d in range(1, NSEC):
            self.term(d).wait_recv()
            own = own + self.terms[d - 1].astype(F32)
        view = piece(self.sum_rows, self.s)
        view[...] = own.astype(BF16)
        for d in range(1, NSEC):
            self.result(d, False).start()

    def terms_finish(self):
        for d in range(1, NSEC):
            self.result(d, True).wait_recv()
        for d in range(1, NSEC):
            self.term(d).wait_send()
            self.result(d, False).wait_send()

    def passing(self, src, dst, d, slot):
        return remote(src, dst, self.psend.at[slot], self.precv.at[slot], to_section(self.s + d))


def kernel(
    hidden_a, hidden_b, mid_b, cotangent, mem_saved, lengths,
    routes_f, routes_b, probs_f, probs_b, gains, w_in, w_out, w_query, w_keyval, w_output,
    rows_out, grads_out, memory_grad_out,
    all_query, all_keyval, all_output, all_shares, all_a, all_x, all_d, part_a, part_b, slopes,
    query, key, value, mixed, middle, upstream, out_rows, grad_rows,
    memory, term_rows, terms, *sems
):
    sems = list(sems)

    def take(count):
        taken = sems[:count]
        del sems[:count]
        return taken

    me, z, y = place()
    my_expert = lax.div(me, NZ)
    section = lax.axis_index("section")
    is_decoder = section >= FIRST_DECODER
    gain_moe = gains[0:1, :]
    gain_att = gains[1:2, :]

    g_wo = Gather(all_output, 0, D, *take(4))
    g_wkv = [Gather(all_keyval, c * INNER, INNER, *take(4)) for c in (0, 1)]
    g_sh = Gather(all_shares, 0, 128, *take(4))
    g_a = [Gather(all_a, *at, *take(4)) for at in halves(CUT_A)]
    g_x = [Gather(all_x, *at, *take(4)) for at in halves(CUT_X)]
    g_d = [Gather(all_d, *at, *take(4)) for at in halves(CUT_D)]
    c_wq = CrossGather(all_query, 0, INNER, *take(4))
    c_a = CrossGather(all_a, CUT_A, D - CUT_A, *take(4))
    c_x = CrossGather(all_x, CUT_X, D - CUT_X, *take(4))
    c_d = CrossGather(all_d, CUT_D, D - CUT_D, *take(4))
    scatter_a = Scatter(CUT_RA, part_a, *take(7))
    scatter_b = Scatter(CUT_RB, part_b, *take(7))
    cross_a = CrossScatter(CUT_RA, part_a, *take(7))
    cross_b = CrossScatter(CUT_RB, part_b, *take(7))
    sections = Sections(memory, term_rows, terms, memory_grad_out, *take(8))

    partners = (
        [to_expert(z + 1, y), to_expert(z - 1, y)]
        + [to_expert(z, y + d) for d in (1, 2, 3)]
        + [to_section(section + d) for d in range(1, NSEC)]
    )
    barrier = pltpu.get_barrier_semaphore()
    for device in partners:
        pl.semaphore_signal(barrier, inc=1, device_id=device, device_id_type=MESH)

    all_output[z, y] = w_output[...]
    all_query[z, y] = w_query[...]
    all_keyval[z, y] = w_keyval[...]
    all_a[z, y] = norm_rows(hidden_a[...], gain_moe)
    all_x[z, y] = norm_rows(hidden_b[...], gain_moe)
    own_shares = all_shares.at[z, y]
    own_shares[...] = jnp.zeros((8, 128), F32)
    for base, routes, probs, line in ((0, routes_f, probs_f, 0), (4, routes_b, probs_b, 2)):
        live = live_row(
            jnp.where(is_decoder, lengths[0, line + 1], lengths[0, line]),
            jnp.where(is_decoder, lengths[1, line + 1], lengths[1, line]),
        )
        for e in range(EXPERTS):
            share = jnp.where(routes[0:1, :] == e, probs[0:1, :], 0.0) + jnp.where(
                routes[1:2, :] == e, probs[1:2, :], 0.0
            )
            own_shares[base + e : base + e + 1, 0:TOK] = share * live
    pl.semaphore_wait(barrier, len(partners))

    def share_column(block, i, base):
        return upright(all_shares[block, i, pl.ds(base + my_expert, 1), 0:TOK])

    def line_rows(ref, block):
        return ref[block].reshape(LINE, D)

    def expert_forward(block, _):
        units = gelu_value(dot_nn(line_rows(all_a, block), w_in[...])).astype(BF16)
        part = dot_nn(units, w_out[...])
        for i in range(NY):
            share = share_column(block, i, 0)
            part_a[block, i] = (part[i * TOK : (i + 1) * TOK] * share).astype(BF16)
        return 0

    def expert_slopes(block, _):
        slopes[block] = gelu_slope(dot_nn(line_rows(all_x, block), w_in[...]))
        return 0

    def expert_backward(block, _):
        for i in range(NY):
            part_b[block, i] = (all_d[block, i].astype(F32) * share_column(block, i, 4)).astype(BF16)
        unit_grad = (dot_nt(line_rows(part_b, block), w_out[...]) * slopes[block]).astype(BF16)
        part_b[block] = dot_nt(unit_grad, w_in[...]).astype(BF16).reshape(NY, TOK, D)
        return 0

    def query_weights():
        return all_query[...].reshape(D, INNER)

    def keyval_weights(first):
        return all_keyval[:, :, :, first : first + INNER].reshape(D, INNER)

    def output_weights():
        return all_output[...].reshape(INNER, D)

    def project_memory(mem_rows):
        key[...] = dot_nn(mem_rows, keyval_weights(0)).astype(BF16)
        value[...] = dot_nn(mem_rows, keyval_weights(INNER)).astype(BF16)

    def project_query(mid_rows):
        query[...] = dot_nn(norm_rows(mid_rows, gain_att), query_weights()).astype(BF16)

    def mix_grads(pairs):
        allowed = allowed_keys(lengths[0, 2], lengths[1, 2])
        for p in pairs:
            at = slice(p * PAIR, (p + 1) * PAIR)
            grads = mix_pair_grad(query[:, at], key[:, at], value[:, at], mixed[:, at], allowed)
            query[:, at], key[:, at], value[:, at] = grads

    def attend_grads():
        d_normed = dot_nt(query[...], query_weights()).astype(BF16).astype(F32)
        d_memory = dot_nt(key[...], keyval_weights(0)) + dot_nt(value[...], keyval_weights(INNER))
        term_rows[...] = jnp.where(is_decoder, d_memory, 0.0).astype(BF16)
        through = norm_grad(mid_b[...], gain_att, d_normed).astype(BF16).astype(F32)
        cot = cotangent[...].astype(F32)
        upstream[...] = jnp.where(is_decoder, cot + through, cot).astype(BF16)
        all_d[z, y] = upstream[...]

    weights, side_a = [g_wo] + g_wkv, [g_sh] + g_a
    crosses = [c_wq, c_a, c_x]

    for g in weights + side_a:
        g.begin()
    for s in range(5):
        for c in crosses:
            c.step(s)
        if s < 3:
            weights[s].step(0)
    for g in weights:
        g.step(1)
    c_wq.begin_line()
    for g in weights:
        g.step(2)
    for g in g_x:
        g.begin()
    c_a.begin_line()
    for g in weights:
        g.step(3)
    for g in side_a:
        g.step(0)
    for g in weights:
        g.step(4)

    for g in side_a:
        g.step(1)
    project_memory(mem_saved[...])
    mixed[...] = dot_nt(cotangent[...], output_weights()).astype(BF16)
    c_wq.arrive()
    project_query(mid_b[...])
    for g in side_a:
        g.step(2)
    mix_grads((0, 1))
    for g in side_a:
        g.step(3)
    for g in g_x:
        g.step(0)
    mix_grads((2, 3))
    attend_grads()
    for g in g_d:
        g.begin()
    c_d.step(0)
    c_x.begin_line()
    sections.terms_begin()
    for g in side_a:
        g.step(4)
    c_d.step(1)

    for g in g_x:
        g.step(1)
    c_a.arrive()
    c_d.step(2)
    lax.fori_loop(0, 2, expert_forward, 0)
    for g in g_x:
        g.step(2)
    c_d.step(3)
    lax.fori_loop(2, 4, expert_forward, 0)
    for g in g_x:
        g.step(3)
    for g in g_d:
        g.step(0)
    c_d.step(4)
    c_d.begin_line()
    lax.fori_loop(4, 6, expert_forward, 0)
    for g in g_x:
        g.step(4)
    lax.fori_loop(6, 8, expert_forward, 0)
    cross_a.begin()

    for s in range(1, 4):
        for g in g_d:
            g.step(s)
        if s == 1:
            c_x.arrive()
            sections.terms_sum()
        lax.fori_loop((0, 0, 2, 5)[s], (0, 2, 5, 8)[s], expert_slopes, 0)
    scatter_a.step(0)
    for g in g_d:
        g.step(4)

    for s in range(1, 4):
        scatter_a.step(s)
        if s == 1:
            c_d.arrive()
            cross_a.sum_line()
        cross_a.step(s - 1)
        lax.fori_loop((0, 0, 3, 6)[s], (0, 3, 6, 8)[s], expert_backward, 0)
    cross_b.begin()
    scatter_b.step(0)
    cross_a.step(3)
    scatter_a.cross()
    cross_a.step(4)

    scatter_b.step(1)
    mixed_a = jnp.concatenate([scatter_a.total(), cross_a.total()], axis=1)
    middle[...] = (hidden_a[...].astype(F32) + mixed_a).astype(BF16)
    sections.spread_root(middle)
    sections.spread_leader()
    scatter_b.step(2)
    sections.spread_wait()
    project_query(middle[...])
    project_memory(memory[...])
    cross_b.sum_line()
    cross_b.step(0)
    allowed = allowed_keys(lengths[0, 0], lengths[1, 0])
    for p in range(INNER // PAIR):
        at = slice(p * PAIR, (p + 1) * PAIR)
        mixed[:, at] = mix_pair(query[:, at], key[:, at], value[:, at], allowed)
    scatter_b.step(3)
    cross_b.step(1)
    projected = jnp.where(is_decoder, dot_nn(mixed[...], output_weights()), 0.0)
    out_rows[...] = (middle[...].astype(F32) + projected).astype(BF16)
    ahead = sections.passing(out_rows, rows_out, 1, 0)
    ahead.start()
    cross_b.step(2)
    cross_b.step(3)
    scatter_b.cross()
    cross_b.step(4)
    sections.terms_finish()
    for g in weights + side_a + g_x + g_d + crosses + [c_d]:
        g.finish()
    scatter_a.finish()
    cross_a.finish()
    sections.spread_finish()
    back = jnp.concatenate([scatter_b.total(), cross_b.total()], axis=1)
    through = norm_grad(hidden_b[...], gain_moe, back)
    grad_rows[...] = (upstream[...].astype(F32) + through).astype(BF16)
    behind = sections.passing(grad_rows, grads_out, -1, 1)
    behind.start()
    scatter_b.finish()
    cross_b.finish()
    ahead.wait()
    behind.wait()


def on_device(
    hidden_fwd,
    hidden_bwd,
    mid_bwd,
    grads_in,
    memory_saved,
    lengths,
    routes_fwd,
    routes_bwd,
    probs_fwd,
    probs_bwd,
    norm_gains,
    w_in,
    w_out,
    w_query,
    w_keyval,
    w_output,
):
    shape = jax.ShapeDtypeStruct((TOK, D), BF16)
    vmem = pl.BlockSpec(memory_space=pltpu.VMEM)
    smem = pl.BlockSpec(memory_space=pltpu.SMEM)
    row_buf = pltpu.VMEM((NZ, NY, TOK, D), BF16)
    tok_buf = pltpu.VMEM((TOK, D), BF16)
    inner_buf = pltpu.VMEM((TOK, INNER), BF16)
    passed_rows, passed_grads, memory_grad = pl.pallas_call(
        kernel,
        out_shape=[shape] * 3,
        in_specs=[vmem] * 5 + [smem] + [vmem] * 10,
        out_specs=[vmem] * 3,
        scratch_shapes=[
            pltpu.VMEM((NZ, NY, 32, INNER), BF16),
            pltpu.VMEM((NZ, NY, 32, 2 * INNER), BF16),
            pltpu.VMEM((NZ, NY, 16, D), BF16),
            pltpu.VMEM((NZ, NY, 8, 128), F32),
            row_buf,
            row_buf,
            row_buf,
            row_buf,
            row_buf,
            pltpu.VMEM((NZ, LINE, UNITS), F32),
            inner_buf,
            inner_buf,
            inner_buf,
            inner_buf,
            tok_buf,
            tok_buf,
            tok_buf,
            tok_buf,
            tok_buf,
            tok_buf,
            pltpu.VMEM((NSEC - 1, PIECE_ROWS, PIECE_COLS), BF16),
        ]
        + GATHER_SEMS * 14
        + scatter_scratch(CUT_RA)
        + scatter_scratch(CUT_RB)
        + cross_scratch(CUT_RA)
        + cross_scratch(CUT_RB)
        + [
            pltpu.SemaphoreType.DMA((6,)),
            pltpu.SemaphoreType.DMA,
            pltpu.SemaphoreType.DMA((NSEC - 1,)),
            pltpu.SemaphoreType.DMA((NSEC - 1,)),
            pltpu.SemaphoreType.DMA((NSEC - 1,)),
            pltpu.SemaphoreType.DMA((NSEC - 1,)),
            pltpu.SemaphoreType.DMA((2,)),
            pltpu.SemaphoreType.DMA((2,)),
        ],
        compiler_params=pltpu.CompilerParams(
            collective_id=0, has_side_effects=True, vmem_limit_bytes=56 * 2**20
        ),
        name="relay_step",
    )(
        hidden_fwd[0],
        hidden_bwd[0],
        mid_bwd[0],
        grads_in[0],
        memory_saved,
        lengths.T,
        routes_fwd[0].T,
        routes_bwd[0].T,
        probs_fwd[0].T,
        probs_bwd[0].T,
        norm_gains[0],
        w_in[0],
        w_out[0],
        w_query[0],
        w_keyval[0],
        w_output[0],
    )
    return (passed_rows[None], passed_grads[None], memory_grad)


def solution(mesh):
    return jax.shard_map(
        on_device,
        mesh=mesh,
        in_specs=(
            P("section", "expert", None),
            P("section", "expert", None),
            P("section", "expert", None),
            P("section", "expert", None),
            P("expert", None),
            P(None, "expert"),
            P("section", "expert", None),
            P("section", "expert", None),
            P("section", "expert", None),
            P("section", "expert", None),
            P("section", None, None),
            P("section", None, "expert"),
            P("section", "expert", None),
            P("section", "expert", None),
            P("section", "expert", None),
            P("section", "expert", None),
        ),
        out_specs=(P("section", "expert", None), P("section", "expert", None), P("expert", None)),
        check_vma=False,
    )
```

time: 301 us -> 259 us (0.86)
  the two profiles are of different devices: /device:TPU:59 before, /device:TPU:49 now
where the time goes in v3:
time: 259 us
  Pallas kernels  255 us (98%)
  local copies, waits for them, and re-layouts  3.21 us (1%)
    pallas_call x1, Pallas kernels, on_device(): pl.pallas_call(kernel, out_shape=[shape] * 3, in_specs=[vmem] * 5 + [smem...  255 us

profile of v3, /device:TPU:49, one launch (start us, length us, event | category | flops | bytes accessed | tf_op | source)
XLA Modules:
  0.0 258.8 jit_solution(8896107300967087091)
XLA Ops:
  0.6 255.0 %relay_step.1 = (bf16[64,1024]{1,0:T(8,128)(2,1)}, bf16[64,1024]{1,0:T(8,128)(2,1)}, bf16[64,1024]{1,0:T(8,128)(2,1)}) custom-call(bf16[64,1024]{1,0:T(8,128)(2,1)} %bitcast.29, bf16[64,1024]{1,0:T(8,128)(2,1)} %bitcast.30, bf16[64,1024]{1,0:T(8,128)(2,1)} %bitcast.31, bf16[64,1024]{1,0:T(8,128)(2,1)} %bitcast.32, bf16[64,1024]{1,0:T(8,128)(2,1)} %mem_saved.1, ...), custom_call_target="tpu_custom_call" | custom-call | tf_op jit(solution)/shard_map/relay_step/pallas_call | solution.py:847
  255.6 0.0 copy-start.1
  255.6 1.6 copy.22
  257.2 0.0 copy-done.1
  257.2 0.0 copy-start
  257.2 0.7 copy.23
  257.9 0.3 copy-done
  258.2 0.7 copy.24
Async XLA Ops:
  255.6 1.6 copy-start.1
  257.2 1.0 copy-start

commit v4 on v3

--- a/solution.py
+++ b/solution.py
@@ -21,7 +21,7 @@
 TOK = 64
 LINE = NY * TOK
 D = 1024
-CUT_A, CUT_X, CUT_D, CUT_RA, CUT_RB = 768, 896, 768, 768, 896
+CUT_A, CUT_X, CUT_D, CUT_RA, CUT_RB = 768, 768, 768, 768, 768
 UNITS = 512
 INNER = 512
 PAIR = 2 * HEAD_DIM
@@ -198,6 +198,45 @@
             self.copy(d, False).wait_send()
 
 
+class RelayLine(Line):
+    def inner(self):
+        return (self.y == 1) | (self.y == 2)
+
+    def begin(self):
+        for d in (1, 3):
+            self.copy(d, False).start()
+
+        @pl.when(jnp.logical_not(self.inner()))
+        def _():
+            self.copy(2, False).start()
+
+    def relay(self):
+        @pl.when(self.y == 1)
+        def _():
+            self.copy(3, True).wait_recv()
+
+        @pl.when(self.y == 2)
+        def _():
+            self.copy(1, True).wait_recv()
+
+        @pl.when(self.inner())
+        def _():
+            block = self.view(NY - 1 - self.y)
+            target = to_expert(self.z, jnp.where(self.y == 1, 0, NY - 1))
+            remote(block, block, self.send.at[1], self.recv.at[1], target).start()
+
+    def arrive(self):
+        self.copy(2, True).wait_recv()
+
+        @pl.when(self.y != 2)
+        def _():
+            self.copy(1, True).wait_recv()
+
+        @pl.when(self.y != 1)
+        def _():
+            self.copy(3, True).wait_recv()
+
+
 def halves(cut):
     first = (cut // 128 + 1) // 2 * 128
     return (0, first), (first, cut - first)
@@ -241,13 +280,16 @@
             return array.at[origin, me_y, pl.ds(half * rows, rows), at]
 
         self.ring = Ring(view, zsend, zrecv)
-        self.line = Line(lambda y: array.at[:, y, :, at], ysend, yrecv)
+        self.line = RelayLine(lambda y: array.at[:, y, :, at], ysend, yrecv)
 
     def step(self, s):
         self.ring.step(s)
 
     def begin_line(self):
         self.line.begin()
+
+    def relay(self):
+        self.line.relay()
 
     def arrive(self):
         self.line.arrive()
@@ -333,10 +375,9 @@
         for d in (1, 2, 3):
             self.copy(d, chunk).start()
 
-    def arrive(self):
-        for chunk in (0, 1):
-            for d in (1, 2, 3):
-                self.copy(d, chunk).wait_recv()
+    def arrive(self, chunk):
+        for d in (1, 2, 3):
+            self.copy(d, chunk).wait_recv()
 
     def finish(self):
         for chunk in (0, 1):
@@ -384,18 +425,19 @@
 class Scatter:
     def __init__(self, cut, src, slots, line_buf, line_slots, zsend, zrecv, ysend, yrecv):
         def part(chunk):
-            return pl.ds(*halves(cut)[chunk])
-
+            return pl.ds(chunk * SEQ, SEQ)
+
+        at = pl.ds(0, cut)
         self.part, self.line_buf, self.line_slots = part, line_buf, line_slots
         self.ring = SumRing(
-            lambda dest, chunk: src.at[dest, :, :, part(chunk)],
-            lambda way, step, chunk: slots.at[way, step, :, :, part(chunk)],
+            lambda dest, chunk: src.at[dest, :, part(chunk), at],
+            lambda way, step, chunk: slots.at[way, step, :, part(chunk)],
             zsend,
             zrecv,
         )
         self.line = SumLine(
-            lambda y, chunk: line_buf.at[y, :, part(chunk)],
-            lambda d, chunk: line_slots.at[d - 1, :, part(chunk)],
+            lambda y, chunk: line_buf.at[y, part(chunk)],
+            lambda d, chunk: line_slots.at[d - 1, part(chunk)],
             ysend,
             yrecv,
         )
@@ -406,14 +448,14 @@
     def cross(self):
         for chunk in (0, 1):
             self.ring.step(4, (chunk,))
-            self.line_buf[:, :, self.part(chunk)] = self.ring.total(chunk).astype(BF16)
+            self.line_buf[:, self.part(chunk)] = self.ring.total(chunk).astype(BF16)
             self.line.begin(chunk)
 
-    def total(self):
-        self.line.arrive()
-        result = self.line_buf[self.line.y].astype(F32)
+    def total(self, chunk):
+        self.line.arrive(chunk)
+        result = self.line_buf[self.line.y, self.part(chunk)].astype(F32)
         for d in (1, 2, 3):
-            result = result + self.line_slots[d - 1].astype(F32)
+            result = result + self.line_slots[d - 1, self.part(chunk)].astype(F32)
         return result
 
     def finish(self):
@@ -442,8 +484,8 @@
     def step(self, s):
         self.ring.step(s)
 
-    def total(self):
-        return jnp.concatenate([self.ring.total(0), self.ring.total(1)], axis=0)
+    def total(self, chunk):
+        return self.ring.total(chunk)
 
     def finish(self):
         self.line.finish()
@@ -611,6 +653,71 @@
     all_output[z, y] = w_output[...]
     all_query[z, y] = w_query[...]
     all_keyval[z, y] = w_keyval[...]
+    pl.semaphore_wait(barrier, len(partners))
+
+    def share_column(block, i, base):
+        return upright(all_shares[block, i, pl.ds(base + my_expert, 1), 0:TOK])
+
+    def line_rows(ref, block):
+        return ref[block].reshape(LINE, D)
+
+    def expert_forward(block, _):
+        units = gelu_value(dot_nn(line_rows(all_a, block), w_in[...])).astype(BF16)
+        part = dot_nn(units, w_out[...])
+        for i in range(NY):
+            share = share_column(block, i, 0)
+            part_a[block, i] = (part[i * TOK : (i + 1) * TOK] * share).astype(BF16)
+        return 0
+
+    def expert_slopes(block, _):
+        slopes[block] = gelu_slope(dot_nn(line_rows(all_x, block), w_in[...]))
+        return 0
+
+    def expert_backward(block, _):
+        for i in range(NY):
+            part_b[block, i] = (all_d[block, i].astype(F32) * share_column(block, i, 4)).astype(BF16)
+        unit_grad = (dot_nt(line_rows(part_b, block), w_out[...]) * slopes[block]).astype(BF16)
+        part_b[block] = dot_nt(unit_grad, w_in[...]).astype(BF16).reshape(NY, TOK, D)
+        return 0
+
+    def query_weights():
+        return all_query[...].reshape(D, INNER)
+
+    def keyval_weights(first):
+        return all_keyval[:, :, :, first : first + INNER].reshape(D, INNER)
+
+    def output_weights():
+        return all_output[...].reshape(INNER, D)
+
+    def project_memory(mem_rows):
+        key[...] = dot_nn(mem_rows, keyval_weights(0)).astype(BF16)
+        value[...] = dot_nn(mem_rows, keyval_weights(INNER)).astype(BF16)
+
+    def project_query(mid_rows):
+        query[...] = dot_nn(norm_rows(mid_rows, gain_att), query_weights()).astype(BF16)
+
+    def mix_grads(pairs):
+        allowed = allowed_keys(lengths[0, 2], lengths[1, 2])
+        for p in pairs:
+            at = slice(p * PAIR, (p + 1) * PAIR)
+            grads = mix_pair_grad(query[:, at], key[:, at], value[:, at], mixed[:, at], allowed)
+            query[:, at], key[:, at], value[:, at] = grads
+
+    def attend_grads():
+        d_normed = dot_nt(query[...], query_weights()).astype(BF16).astype(F32)
+        d_memory = dot_nt(key[...], keyval_weights(0)) + dot_nt(value[...], keyval_weights(INNER))
+        term_rows[...] = jnp.where(is_decoder, d_memory, 0.0).astype(BF16)
+        through = norm_grad(mid_b[...], gain_att, d_normed).astype(BF16).astype(F32)
+        cot = cotangent[...].astype(F32)
+        upstream[...] = jnp.where(is_decoder, cot + through, cot).astype(BF16)
+        all_d[z, y] = upstream[...]
+
+    weights, side_a = [g_wo] + g_wkv, [g_sh] + g_a
+    crosses = [c_wq, c_a, c_x]
+
+    for g in weights:
+        g.begin()
+    c_wq.step(0)
     all_a[z, y] = norm_rows(hidden_a[...], gain_moe)
     all_x[z, y] = norm_rows(hidden_b[...], gain_moe)
     own_shares = all_shares.at[z, y]
@@ -625,75 +732,15 @@
                 routes[1:2, :] == e, probs[1:2, :], 0.0
             )
             own_shares[base + e : base + e + 1, 0:TOK] = share * live
-    pl.semaphore_wait(barrier, len(partners))
-
-    def share_column(block, i, base):
-        return upright(all_shares[block, i, pl.ds(base + my_expert, 1), 0:TOK])
-
-    def line_rows(ref, block):
-        return ref[block].reshape(LINE, D)
-
-    def expert_forward(block, _):
-        units = gelu_value(dot_nn(line_rows(all_a, block), w_in[...])).astype(BF16)
-        part = dot_nn(units, w_out[...])
-        for i in range(NY):
-            share = share_column(block, i, 0)
-            part_a[block, i] = (part[i * TOK : (i + 1) * TOK] * share).astype(BF16)
-        return 0
-
-    def expert_slopes(block, _):
-        slopes[block] = gelu_slope(dot_nn(line_rows(all_x, block), w_in[...]))
-        return 0
-
-    def expert_backward(block, _):
-        for i in range(NY):
-            part_b[block, i] = (all_d[block, i].astype(F32) * share_column(block, i, 4)).astype(BF16)
-        unit_grad = (dot_nt(line_rows(part_b, block), w_out[...]) * slopes[block]).astype(BF16)
-        part_b[block] = dot_nt(unit_grad, w_in[...]).astype(BF16).reshape(NY, TOK, D)
-        return 0
-
-    def query_weights():
-        return all_query[...].reshape(D, INNER)
-
-    def keyval_weights(first):
-        return all_keyval[:, :, :, first : first + INNER].reshape(D, INNER)
-
-    def output_weights():
-        return all_output[...].reshape(INNER, D)
-
-    def project_memory(mem_rows):
-        key[...] = dot_nn(mem_rows, keyval_weights(0)).astype(BF16)
-        value[...] = dot_nn(mem_rows, keyval_weights(INNER)).astype(BF16)
-
-    def project_query(mid_rows):
-        query[...] = dot_nn(norm_rows(mid_rows, gain_att), query_weights()).astype(BF16)
-
-    def mix_grads(pairs):
-        allowed = allowed_keys(lengths[0, 2], lengths[1, 2])
-        for p in pairs:
-            at = slice(p * PAIR, (p + 1) * PAIR)
-            grads = mix_pair_grad(query[:, at], key[:, at], value[:, at], mixed[:, at], allowed)
-            query[:, at], key[:, at], value[:, at] = grads
-
-    def attend_grads():
-        d_normed = dot_nt(query[...], query_weights()).astype(BF16).astype(F32)
-        d_memory = dot_nt(key[...], keyval_weights(0)) + dot_nt(value[...], keyval_weights(INNER))
-        term_rows[...] = jnp.where(is_decoder, d_memory, 0.0).astype(BF16)
-        through = norm_grad(mid_b[...], gain_att, d_normed).astype(BF16).astype(F32)
-        cot = cotangent[...].astype(F32)
-        upstream[...] = jnp.where(is_decoder, cot + through, cot).astype(BF16)
-        all_d[z, y] = upstream[...]
-
-    weights, side_a = [g_wo] + g_wkv, [g_sh] + g_a
-    crosses = [c_wq, c_a, c_x]
-
-    for g in weights + side_a:
+    for g in side_a:
         g.begin()
-    for s in range(5):
+    c_a.step(0)
+    c_x.step(0)
+    for s in range(1, 5):
+        if s < 4:
+            weights[s - 1].step(0)
         for c in crosses:
             c.step(s)
-        if s < 3:
-            weights[s].step(0)
     for g in weights:
         g.step(1)
     c_wq.begin_line()
@@ -708,6 +755,7 @@
         g.step(0)
     for g in weights:
         g.step(4)
+    c_wq.relay()
 
     for g in side_a:
         g.step(1)
@@ -717,6 +765,7 @@
     project_query(mid_b[...])
     for g in side_a:
         g.step(2)
+    c_a.relay()
     mix_grads((0, 1))
     for g in side_a:
         g.step(3)
@@ -740,6 +789,7 @@
     lax.fori_loop(0, 2, expert_forward, 0)
     for g in g_x:
         g.step(2)
+    c_x.relay()
     c_d.step(3)
     lax.fori_loop(2, 4, expert_forward, 0)
     for g in g_x:
@@ -752,7 +802,6 @@
     for g in g_x:
         g.step(4)
     lax.fori_loop(6, 8, expert_forward, 0)
-    cross_a.begin()
 
     for s in range(1, 4):
         for g in g_d:
@@ -760,6 +809,10 @@
         if s == 1:
             c_x.arrive()
             sections.terms_sum()
+        if s == 2:
+            c_d.relay()
+        if s == 3:
+            cross_a.begin()
         lax.fori_loop((0, 0, 2, 5)[s], (0, 2, 5, 8)[s], expert_slopes, 0)
     scatter_a.step(0)
     for g in g_d:
@@ -769,37 +822,40 @@
         scatter_a.step(s)
         if s == 1:
             c_d.arrive()
-            cross_a.sum_line()
-        cross_a.step(s - 1)
         lax.fori_loop((0, 0, 3, 6)[s], (0, 3, 6, 8)[s], expert_backward, 0)
+    scatter_b.step(0)
+    cross_a.sum_line()
+    cross_a.step(0)
+    scatter_a.cross()
     cross_b.begin()
-    scatter_b.step(0)
-    cross_a.step(3)
-    scatter_a.cross()
-    cross_a.step(4)
+    cross_a.step(1)
 
     scatter_b.step(1)
-    mixed_a = jnp.concatenate([scatter_a.total(), cross_a.total()], axis=1)
-    middle[...] = (hidden_a[...].astype(F32) + mixed_a).astype(BF16)
+    for s in (2, 3, 4):
+        cross_a.step(s)
+    for chunk in (0, 1):
+        part = pl.ds(chunk * SEQ, SEQ)
+        mixed_a = jnp.concatenate([scatter_a.total(chunk), cross_a.total(chunk)], axis=1)
+        middle[part] = (hidden_a[part].astype(F32) + mixed_a).astype(BF16)
     sections.spread_root(middle)
+    scatter_b.step(2)
     sections.spread_leader()
-    scatter_b.step(2)
-    sections.spread_wait()
     project_query(middle[...])
-    project_memory(memory[...])
     cross_b.sum_line()
     cross_b.step(0)
+    scatter_b.step(3)
+    sections.spread_wait()
+    project_memory(memory[...])
+    cross_b.step(1)
     allowed = allowed_keys(lengths[0, 0], lengths[1, 0])
     for p in range(INNER // PAIR):
         at = slice(p * PAIR, (p + 1) * PAIR)
         mixed[:, at] = mix_pair(query[:, at], key[:, at], value[:, at], allowed)
-    scatter_b.step(3)
-    cross_b.step(1)
+    cross_b.step(2)
     projected = jnp.where(is_decoder, dot_nn(mixed[...], output_weights()), 0.0)
     out_rows[...] = (middle[...].astype(F32) + projected).astype(BF16)
     ahead = sections.passing(out_rows, rows_out, 1, 0)
     ahead.start()
-    cross_b.step(2)
     cross_b.step(3)
     scatter_b.cross()
     cross_b.step(4)
@@ -809,15 +865,19 @@
     scatter_a.finish()
     cross_a.finish()
     sections.spread_finish()
-    back = jnp.concatenate([scatter_b.total(), cross_b.total()], axis=1)
-    through = norm_grad(hidden_b[...], gain_moe, back)
-    grad_rows[...] = (upstream[...].astype(F32) + through).astype(BF16)
-    behind = sections.passing(grad_rows, grads_out, -1, 1)
-    behind.start()
+    behind = []
+    for chunk in (0, 1):
+        part = pl.ds(chunk * SEQ, SEQ)
+        back = jnp.concatenate([scatter_b.total(chunk), cross_b.total(chunk)], axis=1)
+        through = norm_grad(hidden_b[part], gain_moe, back)
+        grad_rows[part] = (upstream[part].astype(F32) + through).astype(BF16)
+        behind.append(sections.passing(grad_rows.at[part], grads_out.at[part], -1, 1 + chunk))
+        behind[chunk].start()
     scatter_b.finish()
     cross_b.finish()
     ahead.wait()
-    behind.wait()
+    for copy in behind:
+        copy.wait()
 
 
 def on_device(
@@ -884,8 +944,8 @@
             pltpu.SemaphoreType.DMA((NSEC - 1,)),
             pltpu.SemaphoreType.DMA((NSEC - 1,)),
             pltpu.SemaphoreType.DMA((NSEC - 1,)),
-            pltpu.SemaphoreType.DMA((2,)),
-            pltpu.SemaphoreType.DMA((2,)),
+            pltpu.SemaphoreType.DMA((3,)),
+            pltpu.SemaphoreType.DMA((3,)),
         ],
         compiler_params=pltpu.CompilerParams(
             collective_id=0, has_side_effects=True, vmem_limit_bytes=56 * 2**20

time: 259 us -> 251 us (0.969)
  the two profiles are of different devices: /device:TPU:49 before, /device:TPU:59 now
where the time goes in v4:
time: 251 us
  Pallas kernels  247 us (98%)
  local copies, waits for them, and re-layouts  3.21 us (1%)
    pallas_call x1, Pallas kernels, on_device(): pl.pallas_call(kernel, out_shape=[shape] * 3, in_specs=[vmem] * 5 + [smem...  247 us

profile of v4, /device:TPU:59, one launch (start us, length us, event | category | flops | bytes accessed | tf_op | source)
XLA Modules:
  0.0 250.7 jit_solution(12750724756253570115)
XLA Ops:
  0.6 246.9 %relay_step.1 = (bf16[64,1024]{1,0:T(8,128)(2,1)}, bf16[64,1024]{1,0:T(8,128)(2,1)}, bf16[64,1024]{1,0:T(8,128)(2,1)}) custom-call(bf16[64,1024]{1,0:T(8,128)(2,1)} %bitcast.29, bf16[64,1024]{1,0:T(8,128)(2,1)} %bitcast.30, bf16[64,1024]{1,0:T(8,128)(2,1)} %bitcast.31, bf16[64,1024]{1,0:T(8,128)(2,1)} %bitcast.32, bf16[64,1024]{1,0:T(8,128)(2,1)} %mem_saved.1, ...), custom_call_target="tpu_custom_call" | custom-call | tf_op jit(solution)/shard_map/relay_step/pallas_call | solution.py:907
  247.5 0.0 copy-start.1
  247.5 1.6 copy.22
  249.1 0.0 copy-done.1
  249.1 0.0 copy-start
  249.1 0.7 copy.23
  249.8 0.3 copy-done
  250.1 0.7 copy.24
Async XLA Ops:
  247.5 1.6 copy-start.1
  249.1 1.0 copy-start
